TPU v7x, 128 devices: a whole 4x4x4 slice. The times are simulated.
128 devices in a mesh: by: 4 (over y_hi, core), bz: 32 (over x, z, y_lo).
Axes of the slice: x: 4, y: 4 (y_hi: 2, y_lo: 2; y = y_hi * 2 + y_lo), z: 4, core: 2. Of those that a mesh axis runs over, the one named last changes fastest.
Arguments:
- fields: float32 [8, 64, 1024, 512], P(None, 'by', 'bz'), may hold values from -400 to 400
- conductance: float32 [64, 1024, 512], P('by', 'bz'), may hold values from 0.05 to 1
Outputs:
- basis: float32 [8, 64, 1024, 512], P(None, 'by', 'bz')
- factor: float32 [512, 512], replicated
All inputs are finite; a program needn't handle non-finite values.
Results may differ from a plain program's by a relative error of at most 0.0003.
Values sent between devices are 32-bit elements; how exact they have to be, the bound alone decides.
No kernel may reach another device: no remote copies, remote signals or barrier semaphores. Data moves between devices by JAX's collectives and lax.ppermute only.
A program may use at most 320 MiB of HBM per device.

v0:
```python
import jax
import jax.numpy as jnp
from jax import lax
from jax.experimental import pallas as pl
from jax.experimental.pallas import tpu as pltpu
from jax.sharding import Mesh, PartitionSpec as P

HI = lax.Precision.HIGHEST
BLK = 128
PAN = 16
Y_AXES = ("yh", "yl")

def shifted(piece, axes, count, distance):
    return lax.ppermute(piece, axes, [(i, (i + distance) % count) for i in range(count)])


def scatter_sum(pieces, axes, count):
    me = lax.axis_index(axes)
    own = lax.dynamic_index_in_dim(pieces, me, 0, keepdims=False)
    for d in range(1, count):
        send = lax.dynamic_index_in_dim(pieces, (me + d) % count, 0, keepdims=False)
        own = own + shifted(send, axes, count, d)
    return own


def gather(piece, axes, count):
    me = lax.axis_index(axes)
    out = jnp.zeros((count,) + piece.shape, piece.dtype)
    for d in range(count):
        part = piece if d == 0 else shifted(piece, axes, count, d)
        out = lax.dynamic_update_index_in_dim(out, part, (me - d) % count, 0)
    return out


def exchange_sum(piece, axes, count):
    total = piece
    for d in range(1, count):
        total = total + shifted(piece, axes, count, d)
    return total


def sum_over_devices(blocks):
    shape = blocks.shape
    x = blocks.reshape(2, 4, -1, shape[-1])
    x = scatter_sum(x, ("c",), 2)
    x = scatter_sum(x, Y_AXES, 4)
    x = exchange_sum(x, ("z",), 4)
    x = exchange_sum(x, ("x",), 4)
    x = gather(x, Y_AXES, 4)
    x = gather(x, ("c",), 2)
    return x.reshape(shape)


def rows_of(x,k):
    return jnp.broadcast_to(x[k:k+1,:],(8,x.shape[1]))

def diag_factor(work, PAN=PAN):
    nt=PAN//8
    iota=lax.broadcasted_iota(jnp.int32,(8,128),0)
    for p in range(BLK//PAN):
        j=p*PAN
        left=[work[j+8*t:j+8*t+8,0:128] for t in range(nt)]
        right=[work[j+8*t:j+8*t+8,128:256] for t in range(nt)]
        cols=[[jnp.broadcast_to(left[t][:,j+k:j+k+1],(8,128)) for t in range(nt)] for k in range(PAN)]
        scale=[jnp.zeros((8,128),jnp.float32) for _ in range(nt)]
        for k in range(PAN):
            t0,s0=k//8,k%8
            d=rows_of(cols[k][t0],s0)
            inv=1.0/d
            scale[t0]=jnp.where(iota==s0,lax.rsqrt(d),scale[t0])
            coef=[None]*nt
            for t in range(t0,nt):
                c=cols[k][t]*inv
                if t==t0: c=jnp.where(iota>s0,c,0.0)
                coef[t]=c
            for m in range(k+1,PAN):
                b=rows_of(cols[m][t0],s0)
                for t in range(t0,nt):
                    cols[m][t]=cols[m][t]-coef[t]*b
            for arr in (left,right):
                b=rows_of(arr[t0],s0)
                for t in range(t0,nt):
                    arr[t]=arr[t]-coef[t]*b
        left=[l*s for l,s in zip(left,scale)]
        right=[l*s for l,s in zip(right,scale)]
        for t in range(nt):
            work[j+8*t:j+8*t+8,0:128]=left[t]
            work[j+8*t:j+8*t+8,128:256]=right[t]
        if j+PAN<BLK:
            L=jnp.concatenate(left,0)
            R=jnp.concatenate([L,jnp.concatenate(right,0)],1)
            up=lax.dot_general(L,R,(((0,),(0,)),((),())),precision=HI,preferred_element_type=jnp.float32)
            work[j+PAN:BLK,:]=work[j+PAN:BLK,:]-up[j+PAN:BLK,:]

def factor_kernel(g_ref,fac_ref,n_ref,work):
    n=n_ref.shape[0]
    cnt=n//BLK
    t=0
    for i in range(cnt):
        for j in range(i,cnt):
            n_ref[i*BLK:(i+1)*BLK,j*BLK:(j+1)*BLK]=g_ref[t]
            t+=1
    r=lax.broadcasted_iota(jnp.int32,(BLK,BLK),0)
    c=lax.broadcasted_iota(jnp.int32,(BLK,BLK),1)
    for k in range(cnt):
        lo,hi=k*BLK,(k+1)*BLK
        work[:,0:128]=n_ref[lo:hi,lo:hi]
        work[:,128:256]=jnp.where(r==c,1.0,0.0)
        diag_factor(work)
        rkk=jnp.where(r<=c,work[:,0:128],0.0)
        m=jnp.where(r>=c,work[:,128:256],0.0)
        fac_ref[lo:hi,lo:hi]=rkk
        if lo>0:
            fac_ref[lo:hi,0:lo]=jnp.zeros((BLK,lo),jnp.float32)
            n_ref[lo:hi,0:lo]=jnp.dot(m,n_ref[lo:hi,0:lo],precision=HI,preferred_element_type=jnp.float32)
        n_ref[lo:hi,lo:hi]=m
        if hi<n:
            rk=jnp.dot(m,n_ref[lo:hi,hi:n],precision=HI,preferred_element_type=jnp.float32)
            fac_ref[lo:hi,hi:n]=rk
            n_ref[lo:hi,hi:n]=jnp.zeros((BLK,n-hi),jnp.float32)
            upn=lax.dot_general(rk,n_ref[lo:hi,0:hi],(((0,),(0,)),((),())),precision=HI,preferred_element_type=jnp.float32)
            if lo>0: n_ref[hi:n,0:lo]=n_ref[hi:n,0:lo]-upn[:,0:lo]
            n_ref[hi:n,lo:hi]=-upn[:,lo:hi]
            upw=lax.dot_general(rk,rk,(((0,),(0,)),((),())),precision=HI,preferred_element_type=jnp.float32)
            for i in range(k+1,cnt):
                a=i*BLK
                n_ref[a:a+BLK,a:n]=n_ref[a:a+BLK,a:n]-upw[a-hi:a-hi+BLK,a-hi:]


def factor_and_inverse(blocks, n):
    square = jax.ShapeDtypeStruct((n, n), jnp.float32)
    whole = pl.BlockSpec(memory_space=pltpu.VMEM)
    return pl.pallas_call(
        factor_kernel,
        out_shape=(square, square),
        in_specs=[whole],
        out_specs=(whole, whole),
        scratch_shapes=[pltpu.VMEM((BLK, 2 * BLK), jnp.float32)],
        compiler_params=pltpu.CompilerParams(vmem_limit_bytes=32 * 2**20),
    )(blocks)


def ahead(a, axis):
    return pltpu.roll(a, a.shape[axis] - 1, axis)


def behind(a, axis):
    return pltpu.roll(a, 1, axis)


def link(a, b):
    return 0.125 * jnp.sqrt(a * b)


def link_along(k, axis):
    n = k.shape[axis]
    at = lax.broadcasted_iota(jnp.int32, k.shape, axis)
    return jnp.where(at < n - 1, link(k, ahead(k, axis)), 0.0)


def flow_along(u, w, axis):
    flux = w * (ahead(u, axis) - u)
    return flux - behind(flux, axis)


def add_first_row(a, row):
    top = a[0:8]
    at = lax.broadcasted_iota(jnp.int32, top.shape, 0)
    top = top + jnp.where(at == 0, jnp.broadcast_to(row, top.shape), 0.0)
    return jnp.concatenate([top, a[8:]], 0)


def add_last_row(a, row):
    n = a.shape[0]
    end = a[n - 8 :]
    at = lax.broadcasted_iota(jnp.int32, end.shape, 0)
    end = end + jnp.where(at == 7, jnp.broadcast_to(row, end.shape), 0.0)
    return jnp.concatenate([a[: n - 8], end], 0)


def relax_slabs(u, wx, wy, wz, emit):
    count = wx.shape[0]
    below = None
    for y in range(count):
        c = u(y)
        t = flow_along(c, wx[y], 1) + flow_along(c, wz[y], 0)
        if below is not None:
            t = t - below
        if y + 1 < count:
            below = wy[y] * (u(y + 1) - c)
            t = t + below
        emit(y, c, t)


def own_kernel(f_ref, k_ref, p_ref, wx, wy, wz, pzlo, pzhi):
    count, nz, _ = k_ref.shape

    @pl.when(pl.program_id(0) == 0)
    def _():
        for y in range(count):
            k = k_ref[y]
            wx[y] = link_along(k, 1)
            wz[y] = link_along(k, 0)
            wy[y] = link(k, k_ref[y + 1]) if y + 1 < count else jnp.zeros_like(k)

    def emit(y, c, t):
        r = c + t
        p_ref[0, y] = r
        pzlo[0, y : y + 1] = r[0:1]
        pzhi[0, y : y + 1] = r[nz - 1 : nz]

    relax_slabs(lambda y: f_ref[0, y], wx, wy, wz, emit)


def limit(mib):
    return pltpu.CompilerParams(vmem_limit_bytes=mib * 2**20)


def own_relax(fields, conductance):
    nf, ny, nz, nx = fields.shape
    block = pl.BlockSpec((1, ny, nz, nx), lambda f: (f, 0, 0, 0))
    whole = pl.BlockSpec((ny, nz, nx), lambda f: (0, 0, 0))
    zface = pl.BlockSpec((1, ny, nx), lambda f: (f, 0, 0))
    w = jax.ShapeDtypeStruct((ny, nz, nx), jnp.float32)
    zf = jax.ShapeDtypeStruct((nf, ny, nx), jnp.float32)
    return pl.pallas_call(
        own_kernel,
        grid=(nf,),
        in_specs=[block, whole],
        out_specs=(block, whole, whole, whole, zface, zface),
        out_shape=(jax.ShapeDtypeStruct(fields.shape, jnp.float32), w, w, w, zf, zf),
        compiler_params=limit(18),
    )(fields, conductance)


def face_kernel(
    p0, p1, pzlo, pzhi, ylo, yhi, zlo, zhi, yu, yd, zl, zr,
    oylo, oyhi, ozlo, ozhi, lyu, lyd, lzl, lzr,
):
    nf, _, nz, _ = p0.shape
    ny = pzlo.shape[1]
    lyu[...] = link(ylo[nf, 0], yu[nf, 0])
    lyd[...] = link(yhi[nf, 0], yd[nf, 0])
    lzl[...] = link(zlo[nf], zl[nf])
    lzr[...] = link(zhi[nf], zr[nf])
    for f in range(nf):
        up = lyu[...] * (yu[f, 0] - ylo[f, 0])
        down = lyd[...] * (yd[f, 0] - yhi[f, 0])
        left = lzl[...] * (zl[f] - zlo[f])
        right = lzr[...] * (zr[f] - zhi[f])

        def both(a, first, last):
            return add_last_row(add_first_row(a, first), last)

        oylo[f, 0] = both(p0[f, 0] + up, left[0:1], right[0:1])
        oyhi[f, 0] = both(p1[f, 0] + down, left[ny - 1 : ny], right[ny - 1 : ny])
        ozlo[f] = both(pzlo[f] + left, up[0:1], down[0:1])
        ozhi[f] = both(pzhi[f] + right, up[nz - 1 : nz], down[nz - 1 : nz])


def face_relax(p, pzlo, pzhi, ylo, yhi, zlo, zhi, yu, yd, zl, zr):
    nf, ny, nz, nx = p.shape
    full = lambda a: pl.BlockSpec(a.shape, lambda i: (0,) * len(a.shape))
    slab = lambda y: pl.BlockSpec((nf, 1, nz, nx), lambda i: (0, y, 0, 0))
    rest = (pzlo, pzhi, ylo, yhi, zlo, zhi, yu, yd, zl, zr)
    ys = jax.ShapeDtypeStruct((nf, 1, nz, nx), jnp.float32)
    zs = jax.ShapeDtypeStruct((nf, ny, nx), jnp.float32)
    ly = jax.ShapeDtypeStruct((nz, nx), jnp.float32)
    lz = jax.ShapeDtypeStruct((ny, nx), jnp.float32)
    outs = (ys, ys, zs, zs, ly, ly, lz, lz)
    return pl.pallas_call(
        face_kernel,
        grid=(1,),
        in_specs=[slab(0), slab(ny - 1)] + [full(a) for a in rest],
        out_specs=tuple(full(a) for a in outs),
        out_shape=outs,
        compiler_params=limit(20),
    )(p, p, *rest)


def again_kernel(p_ref, wx, wy, wz, oylo, oyhi, ozlo, ozhi, t_ref, once):
    ny, nz, _ = wx.shape
    for y in range(ny):
        if y == 0:
            once[y] = oylo[0, 0]
        elif y == ny - 1:
            once[y] = oyhi[0, 0]
        else:
            once[y] = p_ref[0, y]
            once[y, 0:1] = ozlo[0, y : y + 1]
            once[y, nz - 1 : nz] = ozhi[0, y : y + 1]

    def emit(y, c, t):
        t_ref[0, y] = c + t

    relax_slabs(lambda y: once[y], wx, wy, wz, emit)


def specs(nf, ny, nz, nx):
    block = pl.BlockSpec((1, ny, nz, nx), lambda f: (f, 0, 0, 0))
    yface = pl.BlockSpec((1, 1, nz, nx), lambda f: (f, 0, 0, 0))
    zface = pl.BlockSpec((1, ny, nx), lambda f: (f, 0, 0))
    return block, yface, zface


def again_relax(p, wx, wy, wz, *faces):
    nf, ny, nz, nx = p.shape
    block, yface, zface = specs(*p.shape)
    whole = pl.BlockSpec((ny, nz, nx), lambda f: (0, 0, 0))
    return pl.pallas_call(
        again_kernel,
        grid=(nf,),
        in_specs=[block, whole, whole, whole, yface, yface, zface, zface],
        out_specs=block,
        out_shape=jax.ShapeDtypeStruct(p.shape, jnp.float32),
        scratch_shapes=[pltpu.VMEM((ny, nz, nx), jnp.float32)],
        compiler_params=limit(18),
    )(p, wx, wy, wz, *faces)


def edge_kernel(
    t_ref, oylo, oyhi, ozlo, ozhi, yu, yd, zl, zr, lyu, lyd, lzl, lzr,
    r_ref, g_ref, high, low,
):
    f = pl.program_id(0)
    _, ny, nz, nx = t_ref.shape
    left = lzl[...] * (zl[0] - ozlo[0])
    right = lzr[...] * (zr[0] - ozhi[0])
    for y in range(ny):
        r = t_ref[0, y]
        if y == 0:
            r = r + lyu[...] * (yu[0, 0] - oylo[0, 0])
        if y == ny - 1:
            r = r + lyd[...] * (yd[0, 0] - oyhi[0, 0])
        r = add_first_row(r, left[y : y + 1])
        r = add_last_row(r, right[y : y + 1])
        r_ref[0, y] = r
        h = r.astype(jnp.bfloat16)
        at = pl.ds(pl.multiple_of(f * (ny * nz) + y * nz, nz), nz)
        high[at] = h
        low[at] = (r - h.astype(jnp.float32)).astype(jnp.bfloat16)

    def cross(a, b):
        return lax.dot_general(a, b, (((0,), (0,)), ((), ())), preferred_element_type=jnp.float32)

    @pl.when(f == pl.num_programs(0) - 1)
    def _():
        half = nx // 2
        part = (slice(0, half), slice(half, nx))
        acc_hh, acc_hl = [], []
        for i in range(3):
            a, b = part[i // 2], part[(i + 1) // 2]
            acc_hh.append(cross(high[:, a], high[:, b]) + cross(low[:, a], low[:, b]))
        for i in range(4):
            acc_hl.append(cross(high[:, part[i // 2]], low[:, part[i % 2]]))
        per = half // BLK

        def inner_block(i, j):
            return slice(i % per * BLK, (i % per + 1) * BLK), slice(j % per * BLK, (j % per + 1) * BLK)

        t = 0
        for i in range(2 * per):
            for j in range(i, 2 * per):
                p, q = i // per, j // per
                a, b = inner_block(i, j)
                g_ref[t] = acc_hh[p + q][a, b] + acc_hl[2 * p + q][a, b] + acc_hl[2 * q + p][b, a].T
                t += 1


def edge_relax(t, faces, halos, links):
    nf, ny, nz, nx = t.shape
    block, yface, zface = specs(*t.shape)
    ly = pl.BlockSpec((nz, nx), lambda f: (0, 0))
    lz = pl.BlockSpec((ny, nx), lambda f: (0, 0))
    cnt = nx // BLK
    nb = cnt * (cnt + 1) // 2
    return pl.pallas_call(
        edge_kernel,
        grid=(nf,),
        in_specs=[block] + [yface, yface, zface, zface] * 2 + [ly, ly, lz, lz],
        out_specs=(block, pl.BlockSpec((nb, BLK, BLK), lambda f: (0, 0, 0))),
        out_shape=(
            jax.ShapeDtypeStruct(t.shape, jnp.float32),
            jax.ShapeDtypeStruct((nb, BLK, BLK), jnp.float32),
        ),
        scratch_shapes=[pltpu.VMEM((nf * ny * nz, nx), jnp.bfloat16)] * 2,
        compiler_params=limit(24),
    )(t, *faces, *halos, *links)


def basis_kernel(r_ref, n_ref, o_ref, high, low):
    @pl.when(pl.program_id(0) == 0)
    def _():
        n = n_ref[...]
        h = n.astype(jnp.bfloat16)
        high[...] = h
        low[...] = (n - h.astype(jnp.float32)).astype(jnp.bfloat16)

    r = r_ref[...]
    a = r.astype(jnp.bfloat16)
    b = (r - a.astype(jnp.float32)).astype(jnp.bfloat16)
    width = r.shape[1]
    step = 256
    for lo in range(0, width, step):
        hi = lo + step

        def times(x, m):
            return lax.dot_general(
                x[:, 0:hi], m[lo:hi, 0:hi], (((1,), (1,)), ((), ())), preferred_element_type=jnp.float32
            )

        o_ref[:, lo:hi] = times(a, high) + (times(a, low) + times(b, high))


def basis_of(rows, inverse_t, chunk=512):
    m, nx = rows.shape
    block = pl.BlockSpec((chunk, nx), lambda i: (i, 0))
    return pl.pallas_call(
        basis_kernel,
        grid=(m // chunk,),
        in_specs=[block, pl.BlockSpec((nx, nx), lambda i: (0, 0))],
        out_specs=block,
        out_shape=jax.ShapeDtypeStruct((m, nx), jnp.float32),
        scratch_shapes=[pltpu.VMEM((nx, nx), jnp.bfloat16)] * 2,
        compiler_params=pltpu.CompilerParams(vmem_limit_bytes=14 * 2**20),
    )(rows, inverse_t)

BY = ("yh", "c")
BZ = ("x", "z", "yl")


def axis_count(axes):
    count = 1
    for axis in axes:
        count *= lax.axis_size(axis)
    return count


def from_next(piece, axes, step):
    n = axis_count(axes)
    return lax.ppermute(piece, axes, [(i + step, i) for i in range(n) if 0 <= i + step < n])


def on_device(fields, conductance):
    nfield, ny, nz, width = fields.shape

    def cells(ys, zs):
        return jnp.concatenate([fields[:, ys, zs], conductance[None, ys, zs]], axis=0)

    every = slice(None)
    ylo, yhi = cells(slice(0, 1), every), cells(slice(-1, None), every)
    zlo, zhi = cells(every, 0), cells(every, -1)

    def neighbours(ylo, yhi, zlo, zhi):
        return from_next(yhi, BY, -1), from_next(ylo, BY, 1), from_next(zhi, BZ, -1), from_next(zlo, BZ, 1)

    halo = neighbours(ylo, yhi, zlo, zhi)
    part, wx, wy, wz, pzlo, pzhi = own_relax(fields, conductance)
    out = face_relax(part, pzlo, pzhi, ylo, yhi, zlo, zhi, *halo)
    faces, links = out[:4], out[4:]
    halo = neighbours(*faces)
    twice = again_relax(part, wx, wy, wz, *faces)
    relaxed, blocks = edge_relax(twice, faces, halo, links)
    total_rows = nfield * ny * axis_count(BY) * nz * axis_count(BZ)
    blocks = sum_over_devices(blocks) / jnp.float32(total_rows)
    factor, inverse_t = factor_and_inverse(blocks, width)
    basis = basis_of(relaxed.reshape(-1, width), inverse_t)
    return (basis.reshape(relaxed.shape), factor)


def solution(mesh):
    fine = Mesh(mesh.devices.reshape(2, 2, 4, 4, 2), ("yh", "c", "x", "z", "yl"))
    return jax.shard_map(
        on_device,
        mesh=fine,
        in_specs=(P(None, BY, BZ, None), P(BY, BZ, None)),
        out_specs=(P(None, BY, BZ, None), P()),
        check_vma=False,
    )
```

profile of v0, /device:TPU:1, one launch (start us, length us, event | category | flops | bytes accessed | tf_op | source)
XLA Modules:
  0.0 165.1 jit_solution(8952033012010795673)
XLA Ops:
  3.0 6.2 %collective-permute-start = (f32[9,1,32,512]{3,2,1,0:T(8,128)S(1)}, f32[9,1,32,512]{3,2,1,0:T(8,128)S(1)}, u32[]{:S(2)}, u32[]{:S(2)}) collective-permute-start(f32[9,1,32,512]{3,2,1,0:T(8,128)S(1)} %pad_maximum_fusion.1.yhi), channel_id=1, source_target_pairs={{0,32},{32,64},{64,96},{1,33},{33,65},{65,97},{2,34},{34,66},{66,9... | collective-permute-start | bytes 1769480 | tf_op jit(solution)/shard_map/ppermute | solution.py:441
  11.2 2.8 %fusion.2 = (f32[8,16,1,512]{3,2,1,0:T(1,128)S(1)}, f32[8,16,1,512]{3,2,1,0:T(1,128)S(1)}) fusion(f32[8,16,32,512]{3,2,1,0:T(8,128)} %f_ref.1), kind=kLoop, calls=%fused_computation.27 | loop fusion | bytes 1048576 | tf_op jit(solution)/shard_map/slice | solution.py:448
  15.1 2.3 %collective-permute-start.2 = (f32[9,16,512]{2,1,0:T(8,128)S(1)}, f32[9,16,512]{2,1,0:T(8,128)S(1)}, u32[]{:S(2)}, u32[]{:S(2)}) collective-permute-start(f32[9,16,512]{2,1,0:T(8,128)S(1)} %pad_maximum_fusion.3.zhi), channel_id=1, source_target_pairs={{0,1},{1,2},{2,3},{3,4},{4,5},{5,6},{6,7},{7,8},{8,9},{9,10},{10,1... | collective-permute-start | bytes 884744 | tf_op jit(solution)/shard_map/ppermute | solution.py:441
  18.8 3.4 %copy-done.2 = f32[8,16,32,512]{3,2,1,0:T(8,128)S(1)} copy-done((f32[8,16,32,512]{3,2,1,0:T(8,128)S(1)}, f32[8,16,32,512]{3,2,1,0:T(8,128)}, u32[]{:S(2)}) %copy-start.2) | copy-done | bytes 8388632
  22.2 12.4 %shard_map.41 = (f32[8,16,32,512]{3,2,1,0:T(8,128)S(1)}, f32[16,32,512]{2,1,0:T(8,128)S(1)}, f32[16,32,512]{2,1,0:T(8,128)S(1)}, f32[16,32,512]{2,1,0:T(8,128)S(...) custom-call(f32[8,16,32,512]{3,2,1,0:T(8,128)S(1)} %copy-done.2, f32[16,32,512]{2,1,0:T(8,128)S(1)} %copy-done.5), custom_call_target="tpu_custom_call" | custom-call | tf_op jit(solution)/shard_map/pallas_call | solution.py:226
  37.0 2.9 %copy-done = f32[8,16,32,512]{3,2,1,0:T(8,128)} copy-done((f32[8,16,32,512]{3,2,1,0:T(8,128)}, f32[8,16,32,512]{3,2,1,0:T(8,128)S(1)}, u32[]{:S(2)}) %copy-start) | copy-done | bytes 8388632
  41.2 6.0 %collective-permute-start.4 = (f32[8,1,32,512]{3,2,1,0:T(8,128)S(1)}, f32[8,1,32,512]{3,2,1,0:T(8,128)S(1)}, u32[]{:S(2)}, u32[]{:S(2)}) collective-permute-start(f32[8,1,32,512]{3,2,1,0:T(8,128)S(1)} %get-tuple-element.27.oyhi), channel_id=1, source_target_pairs={{0,32},{32,64},{64,96},{1,33},{33,65},{65,97},{2,34},{34,66},{66,9... | collective-permute-start | bytes 1572872 | tf_op jit(solution)/shard_map/ppermute | solution.py:441
  49.1 3.7 %collective-permute-start.6 = (f32[8,16,512]{2,1,0:T(8,128)S(1)}, f32[8,16,512]{2,1,0:T(8,128)S(1)}, u32[]{:S(2)}, u32[]{:S(2)}) collective-permute-start(f32[8,16,512]{2,1,0:T(8,128)S(1)} %get-tuple-element.29.ozhi), channel_id=1, source_target_pairs={{0,1},{1,2},{2,3},{3,4},{4,5},{5,6},{6,7},{7,8},{8,9},{9,10},{10,1... | collective-permute-start | bytes 786440 | tf_op jit(solution)/shard_map/ppermute | solution.py:441
  54.2 3.4 %copy-done.1 = f32[8,16,32,512]{3,2,1,0:T(8,128)S(1)} copy-done((f32[8,16,32,512]{3,2,1,0:T(8,128)S(1)}, f32[8,16,32,512]{3,2,1,0:T(8,128)}, u32[]{:S(2)}) %copy-start.1) | copy-done | bytes 8388632
  60.0 11.2 %shard_map.43.t_ref = f32[8,16,32,512]{3,2,1,0:T(8,128)S(1)} custom-call(f32[8,16,32,512]{3,2,1,0:T(8,128)S(1)} %copy-done.1, f32[16,32,512]{2,1,0:T(8,128)S(1)} %get-tuple-element.21.wx, f32[16,32,512]{2,1,0:T(8,128)S(1)} %copy-done.7, f32[16,32,512]{2,1,0:T(8,128)S(1)} %copy-done.9, f32[8,1,32,512]{3,2,1,0:T(8,128)S(1)} %get-tuple-element.26.oylo, ...), custom_call_target="tpu_custom_call" | custom-call | tf_op jit(solution)/shard_map/pallas_call | solution.py:310
  71.3 10.8 %shard_map.44 = (f32[8,16,32,512]{3,2,1,0:T(8,128)S(1)}, f32[10,128,128]{2,1,0:T(8,128)S(1)}) custom-call(f32[8,16,32,512]{3,2,1,0:T(8,128)S(1)} %shard_map.43.t_ref, f32[8,1,32,512]{3,2,1,0:T(8,128)S(1)} %get-tuple-element.26.oylo, f32[8,1,32,512]{3,2,1,0:T(8,128)S(1)} %get-tuple-element.27.oyhi, f32[8,16,512]{2,1,0:T(8,128)S(1)} %get-tuple-element.28.ozlo, ...), custom_call_target="tpu_custom_call" | custom-call | tf_op jit(solution)/shard_map/pallas_call | solution.py:377
  82.0 3.4 %copy-done.3 = f32[8,16,32,512]{3,2,1,0:T(8,128)} copy-done((f32[8,16,32,512]{3,2,1,0:T(8,128)}, f32[8,16,32,512]{3,2,1,0:T(8,128)S(1)}, u32[]{:S(2)}) %copy-start.3) | copy-done | bytes 8388632
  87.2 3.9 %collective-permute-start.10 = (f32[160,128]{1,0:T(8,128)S(1)}, f32[160,128]{1,0:T(8,128)S(1)}, u32[]{:S(2)}, u32[]{:S(2)}) collective-permute-start(f32[160,128]{1,0:T(8,128)S(1)} %get-tuple-element.50), channel_id=1, source_target_pairs={{0,64},{1,65},{64,0},{65,1},{2,66},{3,67},{66,2},{67,3},{4,68},{5,... | collective-permute-start | bytes 245768 | tf_op jit(solution)/shard_map/ppermute | solution.py:14
  91.2 2.4 %collective-permute-start.11 = (f32[160,128]{1,0:T(8,128)S(1)}, f32[160,128]{1,0:T(8,128)S(1)}, u32[]{:S(2)}, u32[]{:S(2)}) collective-permute-start(f32[160,128]{1,0:T(8,128)S(1)} %get-tuple-element.49), channel_id=1, source_target_pairs={{0,65},{1,0},{64,1},{65,64},{2,67},{3,2},{66,3},{67,66},{4,69},{5,... | collective-permute-start | bytes 245768 | tf_op jit(solution)/shard_map/ppermute | solution.py:14
  93.8 3.9 %collective-permute-done.11 = f32[160,128]{1,0:T(8,128)S(1)} collective-permute-done((f32[160,128]{1,0:T(8,128)S(1)}, f32[160,128]{1,0:T(8,128)S(1)}, u32[]{:S(2)}, u32[]{:S(2)}) %collective-permute-start.11) | collective-permute-done | bytes 81952 | tf_op jit(solution)/shard_map/ppermute | solution.py:14
  98.1 2.4 %collective-permute-start.12 = (f32[160,128]{1,0:T(8,128)S(1)}, f32[160,128]{1,0:T(8,128)S(1)}, u32[]{:S(2)}, u32[]{:S(2)}) collective-permute-start(f32[160,128]{1,0:T(8,128)S(1)} %fusion.1), channel_id=1, source_target_pairs={{0,2},{2,4},{4,6},{6,0},{1,3},{3,5},{5,7},{7,1},{8,10},{10,12},{12... | collective-permute-start | bytes 245768 | tf_op jit(solution)/shard_map/ppermute | solution.py:14
  100.5 3.3 %collective-permute-start.13 = (f32[160,128]{1,0:T(8,128)S(1)}, f32[160,128]{1,0:T(8,128)S(1)}, u32[]{:S(2)}, u32[]{:S(2)}) collective-permute-start(f32[160,128]{1,0:T(8,128)S(1)} %fusion.1), channel_id=1, source_target_pairs={{0,4},{2,6},{4,0},{6,2},{1,5},{3,7},{5,1},{7,3},{8,12},{10,14},{12... | collective-permute-start | bytes 245768 | tf_op jit(solution)/shard_map/ppermute | solution.py:14
  107.7 2.9 %collective-permute-start.15 = (f32[160,128]{1,0:T(8,128)S(1)}, f32[160,128]{1,0:T(8,128)S(1)}, u32[]{:S(2)}, u32[]{:S(2)}) collective-permute-start(f32[160,128]{1,0:T(8,128)S(1)} %add_add_fusion.1), channel_id=1, source_target_pairs={{0,8},{8,16},{16,24},{24,0},{1,9},{9,17},{17,25},{25,1},{2,10},{10... | collective-permute-start | bytes 245768 | tf_op jit(solution)/shard_map/ppermute | solution.py:14
  110.6 2.5 %collective-permute-start.16 = (f32[160,128]{1,0:T(8,128)S(1)}, f32[160,128]{1,0:T(8,128)S(1)}, u32[]{:S(2)}, u32[]{:S(2)}) collective-permute-start(f32[160,128]{1,0:T(8,128)S(1)} %add_add_fusion.1), channel_id=1, source_target_pairs={{0,16},{8,24},{16,0},{24,8},{1,17},{9,25},{17,1},{25,9},{2,18},{10... | collective-permute-start | bytes 245768 | tf_op jit(solution)/shard_map/ppermute | solution.py:14
  117.4 4.2 %collective-permute-start.19 = (f32[160,128]{1,0:T(8,128)S(1)}, f32[160,128]{1,0:T(8,128)S(1)}, u32[]{:S(2)}, u32[]{:S(2)}) collective-permute-start(f32[160,128]{1,0:T(8,128)S(1)} %get-tuple-element.39), channel_id=1, source_target_pairs={{0,64},{1,65},{64,0},{65,1},{2,66},{3,67},{66,2},{67,3},{4,68},{5,... | collective-permute-start | bytes 245768 | tf_op jit(solution)/shard_map/ppermute | solution.py:14
  125.0 3.9 %collective-permute-start.21 = (f32[4,160,128]{2,1,0:T(8,128)S(1)}, f32[4,160,128]{2,1,0:T(8,128)S(1)}, u32[]{:S(2)}, u32[]{:S(2)}) collective-permute-start(f32[4,160,128]{2,1,0:T(8,128)S(1)} %bitcast_dynamic-update-slice_fusion.2), channel_id=1, source_target_pairs={{0,32},{32,0},{1,33},{33,1},{2,34},{34,2},{3,35},{35,3},{4,36},{36... | collective-permute-start | bytes 983048 | tf_op jit(solution)/shard_map/ppermute | solution.py:14
  130.2 23.4 %shard_map.45 = (f32[512,512]{1,0:T(8,128)}, f32[512,512]{1,0:T(8,128)S(1)}) custom-call(f32[10,128,128]{2,1,0:T(8,128)S(1)} %bitcast.49), custom_call_target="tpu_custom_call" | custom-call | tf_op jit(solution)/shard_map/pallas_call | solution.py:133
  153.6 3.4 %copy-done.4 = f32[8,16,32,512]{3,2,1,0:T(8,128)S(1)} copy-done((f32[8,16,32,512]{3,2,1,0:T(8,128)S(1)}, f32[8,16,32,512]{3,2,1,0:T(8,128)}, u32[]{:S(2)}) %copy-start.4) | copy-done | bytes 8388632
  157.0 8.1 %shard_map.46 = f32[4096,512]{1,0:T(8,128)} custom-call(f32[4096,512]{1,0:T(8,128)S(1)} %bitcast.48, f32[512,512]{1,0:T(8,128)S(1)} %get-tuple-element.36.n_ref), custom_call_target="tpu_custom_call" | custom-call | tf_op jit(solution)/shard_map/pallas_call | solution.py:418
  (80 shorter events, 31.3 us)
Async XLA Ops:
  0.6 18.2 %copy-start.5 = (f32[16,32,512]{2,1,0:T(8,128)S(1)}, f32[16,32,512]{2,1,0:T(8,128)}, u32[]{:S(2)}) copy-start(f32[16,32,512]{2,1,0:T(8,128)} %k_ref.1) | copy-start | bytes 3145732
  3.0 33.6 %collective-permute-start = (f32[9,1,32,512]{3,2,1,0:T(8,128)S(1)}, f32[9,1,32,512]{3,2,1,0:T(8,128)S(1)}, u32[]{:S(2)}, u32[]{:S(2)}) collective-permute-start(f32[9,1,32,512]{3,2,1,0:T(8,128)S(1)} %pad_maximum_fusion.1.yhi), channel_id=1, source_target_pairs={{0,32},{32,64},{64,96},{1,33},{33,65},{65,97},{2,34},{34,66},{66,9... | collective-permute-start | bytes 1769480 | tf_op jit(solution)/shard_map/ppermute | solution.py:441
  9.2 27.4 %collective-permute-start.1 = (f32[9,1,32,512]{3,2,1,0:T(8,128)S(1)}, f32[9,1,32,512]{3,2,1,0:T(8,128)S(1)}, u32[]{:S(2)}, u32[]{:S(2)}) collective-permute-start(f32[9,1,32,512]{3,2,1,0:T(8,128)S(1)} %pad_maximum_fusion.ylo), channel_id=1, source_target_pairs={{32,0},{64,32},{96,64},{33,1},{65,33},{97,65},{34,2},{66,34},{98,6... | collective-permute-start | bytes 1769480 | tf_op jit(solution)/shard_map/ppermute | solution.py:441
  15.1 21.5 %collective-permute-start.2 = (f32[9,16,512]{2,1,0:T(8,128)S(1)}, f32[9,16,512]{2,1,0:T(8,128)S(1)}, u32[]{:S(2)}, u32[]{:S(2)}) collective-permute-start(f32[9,16,512]{2,1,0:T(8,128)S(1)} %pad_maximum_fusion.3.zhi), channel_id=1, source_target_pairs={{0,1},{1,2},{2,3},{3,4},{4,5},{5,6},{6,7},{7,8},{8,9},{9,10},{10,1... | collective-permute-start | bytes 884744 | tf_op jit(solution)/shard_map/ppermute | solution.py:441
  17.5 19.1 %collective-permute-start.3 = (f32[9,16,512]{2,1,0:T(8,128)S(1)}, f32[9,16,512]{2,1,0:T(8,128)S(1)}, u32[]{:S(2)}, u32[]{:S(2)}) collective-permute-start(f32[9,16,512]{2,1,0:T(8,128)S(1)} %pad_maximum_fusion.2.zlo), channel_id=1, source_target_pairs={{1,0},{2,1},{3,2},{4,3},{5,4},{6,5},{7,6},{8,7},{9,8},{10,9},{11,1... | collective-permute-start | bytes 884744 | tf_op jit(solution)/shard_map/ppermute | solution.py:441
  41.2 30.1 %collective-permute-start.4 = (f32[8,1,32,512]{3,2,1,0:T(8,128)S(1)}, f32[8,1,32,512]{3,2,1,0:T(8,128)S(1)}, u32[]{:S(2)}, u32[]{:S(2)}) collective-permute-start(f32[8,1,32,512]{3,2,1,0:T(8,128)S(1)} %get-tuple-element.27.oyhi), channel_id=1, source_target_pairs={{0,32},{32,64},{64,96},{1,33},{33,65},{65,97},{2,34},{34,66},{66,9... | collective-permute-start | bytes 1572872 | tf_op jit(solution)/shard_map/ppermute | solution.py:441
  47.2 24.0 %collective-permute-start.5 = (f32[8,1,32,512]{3,2,1,0:T(8,128)S(1)}, f32[8,1,32,512]{3,2,1,0:T(8,128)}, u32[]{:S(2)}, u32[]{:S(2)}) collective-permute-start(f32[8,1,32,512]{3,2,1,0:T(8,128)S(1)} %get-tuple-element.26.oylo), channel_id=1, source_target_pairs={{32,0},{64,32},{96,64},{33,1},{65,33},{97,65},{34,2},{66,34},{98,6... | collective-permute-start | bytes 1572872 | tf_op jit(solution)/shard_map/ppermute | solution.py:441
  49.1 22.1 %collective-permute-start.6 = (f32[8,16,512]{2,1,0:T(8,128)S(1)}, f32[8,16,512]{2,1,0:T(8,128)S(1)}, u32[]{:S(2)}, u32[]{:S(2)}) collective-permute-start(f32[8,16,512]{2,1,0:T(8,128)S(1)} %get-tuple-element.29.ozhi), channel_id=1, source_target_pairs={{0,1},{1,2},{2,3},{3,4},{4,5},{5,6},{6,7},{7,8},{8,9},{9,10},{10,1... | collective-permute-start | bytes 786440 | tf_op jit(solution)/shard_map/ppermute | solution.py:441
  52.9 18.3 %collective-permute-start.7 = (f32[8,16,512]{2,1,0:T(8,128)S(1)}, f32[8,16,512]{2,1,0:T(8,128)}, u32[]{:S(2)}, u32[]{:S(2)}) collective-permute-start(f32[8,16,512]{2,1,0:T(8,128)S(1)} %get-tuple-element.28.ozlo), channel_id=1, source_target_pairs={{1,0},{2,1},{3,2},{4,3},{5,4},{6,5},{7,6},{8,7},{9,8},{10,9},{11,1... | collective-permute-start | bytes 786440 | tf_op jit(solution)/shard_map/ppermute | solution.py:441
  60.0 11.2 %copy-start.13 = (f32[16,512]{1,0:T(8,128)S(1)}, f32[16,512]{1,0:T(8,128)}, u32[]{:S(2)}) copy-start(f32[16,512]{1,0:T(8,128)} %copy-done.12) | copy-start | bytes 98308
  85.4 1.7 %collective-permute-start.8 = (f32[4,160,128]{2,1,0:T(8,128)S(1)}, f32[4,160,128]{2,1,0:T(8,128)S(1)}, u32[]{:S(2)}, u32[]{:S(2)}) collective-permute-start(f32[4,160,128]{2,1,0:T(8,128)S(1)} %dynamic-slice_bitcast_fusion), channel_id=1, source_target_pairs={{0,32},{32,0},{1,33},{33,1},{2,34},{34,2},{3,35},{35,3},{4,36},{36... | collective-permute-start | bytes 983048 | tf_op jit(solution)/shard_map/ppermute | solution.py:14
  87.2 6.6 %collective-permute-start.10 = (f32[160,128]{1,0:T(8,128)S(1)}, f32[160,128]{1,0:T(8,128)S(1)}, u32[]{:S(2)}, u32[]{:S(2)}) collective-permute-start(f32[160,128]{1,0:T(8,128)S(1)} %get-tuple-element.50), channel_id=1, source_target_pairs={{0,64},{1,65},{64,0},{65,1},{2,66},{3,67},{66,2},{67,3},{4,68},{5,... | collective-permute-start | bytes 245768 | tf_op jit(solution)/shard_map/ppermute | solution.py:14
  91.2 6.6 %collective-permute-start.11 = (f32[160,128]{1,0:T(8,128)S(1)}, f32[160,128]{1,0:T(8,128)S(1)}, u32[]{:S(2)}, u32[]{:S(2)}) collective-permute-start(f32[160,128]{1,0:T(8,128)S(1)} %get-tuple-element.49), channel_id=1, source_target_pairs={{0,65},{1,0},{64,1},{65,64},{2,67},{3,2},{66,3},{67,66},{4,69},{5,... | collective-permute-start | bytes 245768 | tf_op jit(solution)/shard_map/ppermute | solution.py:14
  93.6 4.5 %collective-permute-start.9 = (f32[160,128]{1,0:T(8,128)S(1)}, f32[160,128]{1,0:T(8,128)S(1)}, u32[]{:S(2)}, u32[]{:S(2)}) collective-permute-start(f32[160,128]{1,0:T(8,128)S(1)} %get-tuple-element.48), channel_id=1, source_target_pairs={{0,1},{1,64},{64,65},{65,0},{2,3},{3,66},{66,67},{67,2},{4,5},{5,6... | collective-permute-start | bytes 245768 | tf_op jit(solution)/shard_map/ppermute | solution.py:14
  98.1 6.4 %collective-permute-start.12 = (f32[160,128]{1,0:T(8,128)S(1)}, f32[160,128]{1,0:T(8,128)S(1)}, u32[]{:S(2)}, u32[]{:S(2)}) collective-permute-start(f32[160,128]{1,0:T(8,128)S(1)} %fusion.1), channel_id=1, source_target_pairs={{0,2},{2,4},{4,6},{6,0},{1,3},{3,5},{5,7},{7,1},{8,10},{10,12},{12... | collective-permute-start | bytes 245768 | tf_op jit(solution)/shard_map/ppermute | solution.py:14
  100.5 6.1 %collective-permute-start.13 = (f32[160,128]{1,0:T(8,128)S(1)}, f32[160,128]{1,0:T(8,128)S(1)}, u32[]{:S(2)}, u32[]{:S(2)}) collective-permute-start(f32[160,128]{1,0:T(8,128)S(1)} %fusion.1), channel_id=1, source_target_pairs={{0,4},{2,6},{4,0},{6,2},{1,5},{3,7},{5,1},{7,3},{8,12},{10,14},{12... | collective-permute-start | bytes 245768 | tf_op jit(solution)/shard_map/ppermute | solution.py:14
  103.8 3.9 %collective-permute-start.14 = (f32[160,128]{1,0:T(8,128)S(1)}, f32[160,128]{1,0:T(8,128)S(1)}, u32[]{:S(2)}, u32[]{:S(2)}) collective-permute-start(f32[160,128]{1,0:T(8,128)S(1)} %fusion.1), channel_id=1, source_target_pairs={{0,6},{2,0},{4,2},{6,4},{1,7},{3,1},{5,3},{7,5},{8,14},{10,8},{12,... | collective-permute-start | bytes 245768 | tf_op jit(solution)/shard_map/ppermute | solution.py:14
  107.7 6.5 %collective-permute-start.15 = (f32[160,128]{1,0:T(8,128)S(1)}, f32[160,128]{1,0:T(8,128)S(1)}, u32[]{:S(2)}, u32[]{:S(2)}) collective-permute-start(f32[160,128]{1,0:T(8,128)S(1)} %add_add_fusion.1), channel_id=1, source_target_pairs={{0,8},{8,16},{16,24},{24,0},{1,9},{9,17},{17,25},{25,1},{2,10},{10... | collective-permute-start | bytes 245768 | tf_op jit(solution)/shard_map/ppermute | solution.py:14
  110.6 5.2 %collective-permute-start.16 = (f32[160,128]{1,0:T(8,128)S(1)}, f32[160,128]{1,0:T(8,128)S(1)}, u32[]{:S(2)}, u32[]{:S(2)}) collective-permute-start(f32[160,128]{1,0:T(8,128)S(1)} %add_add_fusion.1), channel_id=1, source_target_pairs={{0,16},{8,24},{16,0},{24,8},{1,17},{9,25},{17,1},{25,9},{2,18},{10... | collective-permute-start | bytes 245768 | tf_op jit(solution)/shard_map/ppermute | solution.py:14
  113.1 3.6 %collective-permute-start.17 = (f32[160,128]{1,0:T(8,128)S(1)}, f32[160,128]{1,0:T(8,128)S(1)}, u32[]{:S(2)}, u32[]{:S(2)}) collective-permute-start(f32[160,128]{1,0:T(8,128)S(1)} %add_add_fusion.1), channel_id=1, source_target_pairs={{0,24},{8,0},{16,8},{24,16},{1,25},{9,1},{17,9},{25,17},{2,26},{10... | collective-permute-start | bytes 245768 | tf_op jit(solution)/shard_map/ppermute | solution.py:14
  116.7 6.8 %collective-permute-start.18 = (f32[160,128]{1,0:T(8,128)S(1)}, f32[160,128]{1,0:T(8,128)S(1)}, u32[]{:S(2)}, u32[]{:S(2)}) collective-permute-start(f32[160,128]{1,0:T(8,128)S(1)} %get-tuple-element.39), channel_id=1, source_target_pairs={{0,1},{1,64},{64,65},{65,0},{2,3},{3,66},{66,67},{67,2},{4,5},{5,6... | collective-permute-start | bytes 245768 | tf_op jit(solution)/shard_map/ppermute | solution.py:14
  117.4 6.7 %collective-permute-start.19 = (f32[160,128]{1,0:T(8,128)S(1)}, f32[160,128]{1,0:T(8,128)S(1)}, u32[]{:S(2)}, u32[]{:S(2)}) collective-permute-start(f32[160,128]{1,0:T(8,128)S(1)} %get-tuple-element.39), channel_id=1, source_target_pairs={{0,64},{1,65},{64,0},{65,1},{2,66},{3,67},{66,2},{67,3},{4,68},{5,... | collective-permute-start | bytes 245768 | tf_op jit(solution)/shard_map/ppermute | solution.py:14
  121.6 3.4 %collective-permute-start.20 = (f32[160,128]{1,0:T(8,128)S(1)}, f32[160,128]{1,0:T(8,128)S(1)}, u32[]{:S(2)}, u32[]{:S(2)}) collective-permute-start(f32[160,128]{1,0:T(8,128)S(1)} %get-tuple-element.39), channel_id=1, source_target_pairs={{0,65},{1,0},{64,1},{65,64},{2,67},{3,2},{66,3},{67,66},{4,69},{5,... | collective-permute-start | bytes 245768 | tf_op jit(solution)/shard_map/ppermute | solution.py:14
  125.0 5.1 %collective-permute-start.21 = (f32[4,160,128]{2,1,0:T(8,128)S(1)}, f32[4,160,128]{2,1,0:T(8,128)S(1)}, u32[]{:S(2)}, u32[]{:S(2)}) collective-permute-start(f32[4,160,128]{2,1,0:T(8,128)S(1)} %bitcast_dynamic-update-slice_fusion.2), channel_id=1, source_target_pairs={{0,32},{32,0},{1,33},{33,1},{2,34},{34,2},{3,35},{35,3},{4,36},{36... | collective-permute-start | bytes 983048 | tf_op jit(solution)/shard_map/ppermute | solution.py:14
  (12 other events, 33.8 us)
where the time goes:
time: 166 us; the launch traced here: 165 us
  Pallas kernels  66.2 us (40%)
  starting transfers between devices  55 us (33%)
  local copies, waits for them, and re-layouts  28.5 us (17%)
  waiting for transfers between devices  14 us (8%)
    ppermute x14, starting transfers between devices, shifted(): lax.ppermute(piece, axes, [(i, (i + distance) % count) for i in range(cou...  30.3 us
    ppermute x8, starting transfers between devices, from_next(): lax.ppermute(piece, axes, [(i + step, i) for i in range(n) if 0 <= i + st...  24.7 us
    pallas_call x1, Pallas kernels, factor_and_inverse(): pl.pallas_call(factor_kernel, out_shape=(square, square), in_specs=[whole...  23.4 us
    unnamed x32, local copies, waits for them, and re-layouts  22.1 us
    ppermute x14, waiting for transfers between devices, shifted(): lax.ppermute(piece, axes, [(i, (i + distance) % count) for i in range(cou...  14 us
    pallas_call x1, Pallas kernels, own_relax(): pl.pallas_call(own_kernel, grid=(nf,), in_specs=[block, whole], out_specs...  12.4 us
    pallas_call x1, Pallas kernels, again_relax(): pl.pallas_call(again_kernel, grid=(nf,), in_specs=[block, whole, whole, w...  11.2 us
    pallas_call x1, Pallas kernels, edge_relax(): pl.pallas_call(edge_kernel, grid=(nf,), in_specs=[block] + [yface, yface,...  10.8 us
  transfers between devices with their start and end apart: 22, of which 10 were waited for; matrix products, arithmetic and copies ran while one was open for 2% of the time, Pallas kernels for 14%

commit v1 on v0

--- a/solution.py
+++ b/solution.py
@@ -7,7 +7,7 @@
 
 HI = lax.Precision.HIGHEST
 BLK = 128
-PAN = 16
+PAN = 32
 Y_AXES = ("yh", "yl")
 
 def shifted(piece, axes, count, distance):
@@ -136,7 +136,7 @@
         in_specs=[whole],
         out_specs=(whole, whole),
         scratch_shapes=[pltpu.VMEM((BLK, 2 * BLK), jnp.float32)],
-        compiler_params=pltpu.CompilerParams(vmem_limit_bytes=32 * 2**20),
+        compiler_params=pltpu.CompilerParams(vmem_limit_bytes=24 * 2**20),
     )(blocks)
 
 
@@ -192,7 +192,7 @@
         emit(y, c, t)
 
 
-def own_kernel(f_ref, k_ref, p_ref, wx, wy, wz, pzlo, pzhi):
+def own_kernel(f_ref, k_ref, p_ref, wx, wy, wz, pylo, pyhi, pzlo, pzhi):
     count, nz, _ = k_ref.shape
 
     @pl.when(pl.program_id(0) == 0)
@@ -206,10 +206,18 @@
     def emit(y, c, t):
         r = c + t
         p_ref[0, y] = r
+        if y == 0:
+            pylo[0, 0] = r
+        if y == count - 1:
+            pyhi[0, 0] = r
         pzlo[0, y : y + 1] = r[0:1]
         pzhi[0, y : y + 1] = r[nz - 1 : nz]
 
     relax_slabs(lambda y: f_ref[0, y], wx, wy, wz, emit)
+
+
+def far(x):
+    return pltpu.with_memory_space_constraint(x, pltpu.HBM)
 
 
 def limit(mib):
@@ -221,23 +229,25 @@
     block = pl.BlockSpec((1, ny, nz, nx), lambda f: (f, 0, 0, 0))
     whole = pl.BlockSpec((ny, nz, nx), lambda f: (0, 0, 0))
     zface = pl.BlockSpec((1, ny, nx), lambda f: (f, 0, 0))
-    w = jax.ShapeDtypeStruct((ny, nz, nx), jnp.float32)
+    w = pltpu.HBM((ny, nz, nx), jnp.float32)
+    yf = jax.ShapeDtypeStruct((nf, 1, nz, nx), jnp.float32)
+    yface = pl.BlockSpec((1, 1, nz, nx), lambda f: (f, 0, 0, 0))
     zf = jax.ShapeDtypeStruct((nf, ny, nx), jnp.float32)
     return pl.pallas_call(
         own_kernel,
         grid=(nf,),
         in_specs=[block, whole],
-        out_specs=(block, whole, whole, whole, zface, zface),
-        out_shape=(jax.ShapeDtypeStruct(fields.shape, jnp.float32), w, w, w, zf, zf),
-        compiler_params=limit(18),
-    )(fields, conductance)
+        out_specs=(block, whole, whole, whole, yface, yface, zface, zface),
+        out_shape=(pltpu.HBM(fields.shape, jnp.float32), w, w, w, yf, yf, zf, zf),
+        compiler_params=limit(24),
+    )(far(fields), far(conductance))
 
 
 def face_kernel(
-    p0, p1, pzlo, pzhi, ylo, yhi, zlo, zhi, yu, yd, zl, zr,
+    pylo, pyhi, pzlo, pzhi, ylo, yhi, zlo, zhi, yu, yd, zl, zr,
     oylo, oyhi, ozlo, ozhi, lyu, lyd, lzl, lzr,
 ):
-    nf, _, nz, _ = p0.shape
+    nf, _, nz, _ = pylo.shape
     ny = pzlo.shape[1]
     lyu[...] = link(ylo[nf, 0], yu[nf, 0])
     lyd[...] = link(yhi[nf, 0], yd[nf, 0])
@@ -252,17 +262,16 @@
         def both(a, first, last):
             return add_last_row(add_first_row(a, first), last)
 
-        oylo[f, 0] = both(p0[f, 0] + up, left[0:1], right[0:1])
-        oyhi[f, 0] = both(p1[f, 0] + down, left[ny - 1 : ny], right[ny - 1 : ny])
+        oylo[f, 0] = both(pylo[f, 0] + up, left[0:1], right[0:1])
+        oyhi[f, 0] = both(pyhi[f, 0] + down, left[ny - 1 : ny], right[ny - 1 : ny])
         ozlo[f] = both(pzlo[f] + left, up[0:1], down[0:1])
         ozhi[f] = both(pzhi[f] + right, up[nz - 1 : nz], down[nz - 1 : nz])
 
 
-def face_relax(p, pzlo, pzhi, ylo, yhi, zlo, zhi, yu, yd, zl, zr):
-    nf, ny, nz, nx = p.shape
+def face_relax(*args):
+    nf, _, nz, nx = args[0].shape
+    ny = args[2].shape[1]
     full = lambda a: pl.BlockSpec(a.shape, lambda i: (0,) * len(a.shape))
-    slab = lambda y: pl.BlockSpec((nf, 1, nz, nx), lambda i: (0, y, 0, 0))
-    rest = (pzlo, pzhi, ylo, yhi, zlo, zhi, yu, yd, zl, zr)
     ys = jax.ShapeDtypeStruct((nf, 1, nz, nx), jnp.float32)
     zs = jax.ShapeDtypeStruct((nf, ny, nx), jnp.float32)
     ly = jax.ShapeDtypeStruct((nz, nx), jnp.float32)
@@ -271,11 +280,11 @@
     return pl.pallas_call(
         face_kernel,
         grid=(1,),
-        in_specs=[slab(0), slab(ny - 1)] + [full(a) for a in rest],
+        in_specs=[full(a) for a in args],
         out_specs=tuple(full(a) for a in outs),
         out_shape=outs,
-        compiler_params=limit(20),
-    )(p, p, *rest)
+        compiler_params=limit(24),
+    )(*args)
 
 
 def again_kernel(p_ref, wx, wy, wz, oylo, oyhi, ozlo, ozhi, t_ref, once):
@@ -314,8 +323,8 @@
         out_specs=block,
         out_shape=jax.ShapeDtypeStruct(p.shape, jnp.float32),
         scratch_shapes=[pltpu.VMEM((ny, nz, nx), jnp.float32)],
-        compiler_params=limit(18),
-    )(p, wx, wy, wz, *faces)
+        compiler_params=limit(24),
+    )(far(p), far(wx), far(wy), far(wz), *faces)
 
 
 def edge_kernel(
@@ -380,7 +389,7 @@
         in_specs=[block] + [yface, yface, zface, zface] * 2 + [ly, ly, lz, lz],
         out_specs=(block, pl.BlockSpec((nb, BLK, BLK), lambda f: (0, 0, 0))),
         out_shape=(
-            jax.ShapeDtypeStruct(t.shape, jnp.float32),
+            pltpu.HBM(t.shape, jnp.float32),
             jax.ShapeDtypeStruct((nb, BLK, BLK), jnp.float32),
         ),
         scratch_shapes=[pltpu.VMEM((nf * ny * nz, nx), jnp.bfloat16)] * 2,
@@ -422,8 +431,8 @@
         out_specs=block,
         out_shape=jax.ShapeDtypeStruct((m, nx), jnp.float32),
         scratch_shapes=[pltpu.VMEM((nx, nx), jnp.bfloat16)] * 2,
-        compiler_params=pltpu.CompilerParams(vmem_limit_bytes=14 * 2**20),
-    )(rows, inverse_t)
+        compiler_params=pltpu.CompilerParams(vmem_limit_bytes=24 * 2**20),
+    )(far(rows), inverse_t)
 
 BY = ("yh", "c")
 BZ = ("x", "z", "yl")
@@ -455,8 +464,8 @@
         return from_next(yhi, BY, -1), from_next(ylo, BY, 1), from_next(zhi, BZ, -1), from_next(zlo, BZ, 1)
 
     halo = neighbours(ylo, yhi, zlo, zhi)
-    part, wx, wy, wz, pzlo, pzhi = own_relax(fields, conductance)
-    out = face_relax(part, pzlo, pzhi, ylo, yhi, zlo, zhi, *halo)
+    part, wx, wy, wz, *own = own_relax(fields, conductance)
+    out = face_relax(*own, ylo, yhi, zlo, zhi, *halo)
     faces, links = out[:4], out[4:]
     halo = neighbours(*faces)
     twice = again_relax(part, wx, wy, wz, *faces)

time: 166 us -> 156 us (0.940)
  local copies, waits for them, and re-layouts: 28.5 us -> 10.4 us
  Pallas kernels: 66.2 us -> 73.9 us
    unnamed x32 -> x24, local copies, waits for them, and re-layouts: 22.1 us -> 4.14 us
    pallas_call x1, Pallas kernels: 12.4 us -> 15.9 us  [own_relax(): pl.pallas_call(own_kernel, grid=(nf,), in_specs=[block, whole], out_specs...]
    pallas_call x1, Pallas kernels: 8.13 us -> 11.5 us  [basis_of(): pl.pallas_call(basis_kernel, grid=(m // chunk,), in_specs=[block, pl.Bloc...]
    pallas_call x1, Pallas kernels: 11.2 us -> 13.5 us  [again_relax(): pl.pallas_call(again_kernel, grid=(nf,), in_specs=[block, whole, whole, w...]
    pallas_call x1, Pallas kernels: 23.4 us -> 21.1 us  [factor_and_inverse(): pl.pallas_call(factor_kernel, out_shape=(square, square), in_specs=[whole...]
  transfers between devices with their start and end apart: 22 -> 22, of which waited for: 10 -> 11; matrix products, arithmetic and copies ran while one was open for 2% -> 3% of each run, Pallas kernels for 14% -> 19%
where the time goes in v1:
time: 156 us; the launch traced here: 155 us
  Pallas kernels  73.9 us (47%)
  starting transfers between devices  55.4 us (36%)
  waiting for transfers between devices  13.7 us (9%)
  local copies, waits for them, and re-layouts  10.4 us (7%)
    ppermute x14, starting transfers between devices, shifted(): lax.ppermute(piece, axes, [(i, (i + distance) % count) for i in range(cou...  30.6 us
    ppermute x8, starting transfers between devices, from_next(): lax.ppermute(piece, axes, [(i + step, i) for i in range(n) if 0 <= i + st...  24.7 us
    pallas_call x1, Pallas kernels, factor_and_inverse(): pl.pallas_call(factor_kernel, out_shape=(square, square), in_specs=[whole...  21.1 us
    pallas_call x1, Pallas kernels, own_relax(): pl.pallas_call(own_kernel, grid=(nf,), in_specs=[block, whole], out_specs...  15.9 us
    ppermute x14, waiting for transfers between devices, shifted(): lax.ppermute(piece, axes, [(i, (i + distance) % count) for i in range(cou...  13.6 us
    pallas_call x1, Pallas kernels, again_relax(): pl.pallas_call(again_kernel, grid=(nf,), in_specs=[block, whole, whole, w...  13.5 us
    pallas_call x1, Pallas kernels, basis_of(): pl.pallas_call(basis_kernel, grid=(m // chunk,), in_specs=[block, pl.Bloc...  11.5 us
    pallas_call x1, Pallas kernels, edge_relax(): pl.pallas_call(edge_kernel, grid=(nf,), in_specs=[block] + [yface, yface,...  11.5 us
  transfers between devices with their start and end apart: 22, of which 11 were waited for; matrix products, arithmetic and copies ran while one was open for 3% of the time, Pallas kernels for 19%

profile of v1, /device:TPU:1, one launch (start us, length us, event | category | flops | bytes accessed | tf_op | source)
XLA Modules:
  0.0 154.7 jit_solution(8940536850708554180)
XLA Ops:
  2.9 6.2 %collective-permute-start = (f32[9,1,32,512]{3,2,1,0:T(8,128)S(1)}, f32[9,1,32,512]{3,2,1,0:T(8,128)S(1)}, u32[]{:S(2)}, u32[]{:S(2)}) collective-permute-start(f32[9,1,32,512]{3,2,1,0:T(8,128)S(1)} %pad_maximum_fusion.1.yhi), channel_id=1, source_target_pairs={{0,32},{32,64},{64,96},{1,33},{33,65},{65,97},{2,34},{34,66},{66,9... | collective-permute-start | bytes 1769480 | tf_op jit(solution)/shard_map/ppermute | solution.py:450
  9.1 1.9 %collective-permute-start.1 = (f32[9,1,32,512]{3,2,1,0:T(8,128)S(1)}, f32[9,1,32,512]{3,2,1,0:T(8,128)S(1)}, u32[]{:S(2)}, u32[]{:S(2)}) collective-permute-start(f32[9,1,32,512]{3,2,1,0:T(8,128)S(1)} %pad_maximum_fusion.ylo), channel_id=1, source_target_pairs={{32,0},{64,32},{96,64},{33,1},{65,33},{97,65},{34,2},{66,34},{98,6... | collective-permute-start | bytes 1769480 | tf_op jit(solution)/shard_map/ppermute | solution.py:450
  11.1 2.8 %fusion.2 = (f32[8,16,1,512]{3,2,1,0:T(1,128)S(1)}, f32[8,16,1,512]{3,2,1,0:T(1,128)S(1)}) fusion(f32[8,16,32,512]{3,2,1,0:T(8,128)} %f_ref.1), kind=kLoop, calls=%fused_computation.27 | loop fusion | bytes 1048576 | tf_op jit(solution)/shard_map/slice | solution.py:457
  15.0 2.3 %collective-permute-start.2 = (f32[9,16,512]{2,1,0:T(8,128)S(1)}, f32[9,16,512]{2,1,0:T(8,128)S(1)}, u32[]{:S(2)}, u32[]{:S(2)}) collective-permute-start(f32[9,16,512]{2,1,0:T(8,128)S(1)} %pad_maximum_fusion.3.zhi), channel_id=1, source_target_pairs={{0,1},{1,2},{2,3},{3,4},{4,5},{5,6},{6,7},{7,8},{8,9},{9,10},{10,1... | collective-permute-start | bytes 884744 | tf_op jit(solution)/shard_map/ppermute | solution.py:450
  18.7 15.9 %shard_map.41 = (f32[8,16,32,512]{3,2,1,0:T(8,128)}, f32[16,32,512]{2,1,0:T(8,128)}, f32[16,32,512]{2,1,0:T(8,128)}, f32[16,32,512]{2,1,0:T(8,128)}, f32[8,1,32,...) custom-call(f32[8,16,32,512]{3,2,1,0:T(8,128)} %f_ref.1, ...), custom_call_target="tpu_custom_call" | custom-call | tf_op jit(solution)/shard_map/pallas_call | solution.py:236
  37.5 6.0 %collective-permute-start.4 = (f32[8,1,32,512]{3,2,1,0:T(8,128)S(1)}, f32[8,1,32,512]{3,2,1,0:T(8,128)S(1)}, u32[]{:S(2)}, u32[]{:S(2)}) collective-permute-start(f32[8,1,32,512]{3,2,1,0:T(8,128)S(1)} %get-tuple-element.31.oyhi), channel_id=1, source_target_pairs={{0,32},{32,64},{64,96},{1,33},{33,65},{65,97},{2,34},{34,66},{66,9... | collective-permute-start | bytes 1572872 | tf_op jit(solution)/shard_map/ppermute | solution.py:450
  43.5 1.9 %collective-permute-start.5 = (f32[8,1,32,512]{3,2,1,0:T(8,128)S(1)}, f32[8,1,32,512]{3,2,1,0:T(8,128)S(1)}, u32[]{:S(2)}, u32[]{:S(2)}) collective-permute-start(f32[8,1,32,512]{3,2,1,0:T(8,128)S(1)} %get-tuple-element.30.oylo), channel_id=1, source_target_pairs={{32,0},{64,32},{96,64},{33,1},{65,33},{97,65},{34,2},{66,34},{98,6... | collective-permute-start | bytes 1572872 | tf_op jit(solution)/shard_map/ppermute | solution.py:450
  45.4 3.7 %collective-permute-start.6 = (f32[8,16,512]{2,1,0:T(8,128)S(1)}, f32[8,16,512]{2,1,0:T(8,128)S(1)}, u32[]{:S(2)}, u32[]{:S(2)}) collective-permute-start(f32[8,16,512]{2,1,0:T(8,128)S(1)} %get-tuple-element.33.ozhi), channel_id=1, source_target_pairs={{0,1},{1,2},{2,3},{3,4},{4,5},{5,6},{6,7},{7,8},{8,9},{9,10},{10,1... | collective-permute-start | bytes 786440 | tf_op jit(solution)/shard_map/ppermute | solution.py:450
  50.6 13.5 %shard_map.43.t_ref = f32[8,16,32,512]{3,2,1,0:T(8,128)S(1)} custom-call(f32[8,16,32,512]{3,2,1,0:T(8,128)} %get-tuple-element.22.p_ref, f32[16,32,512]{2,1,0:T(8,128)} %get-tuple-element.23.wx, f32[16,32,512]{2,1,0:T(8,128)} %get-tuple-element.24.wy, f32[16,32,512]{2,1,0:T(8,128)} %get-tuple-element.25.wz, f32[8,1,32,512]{3,2,1,0:T(8,128)S(1)} %get-tuple-element.30.oylo, ...), custom_call_target="tpu_custom_call" | custom-call | tf_op jit(solution)/shard_map/pallas_call | solution.py:319
  65.8 11.5 %shard_map.44 = (f32[8,16,32,512]{3,2,1,0:T(8,128)}, f32[10,128,128]{2,1,0:T(8,128)S(1)}) custom-call(f32[8,16,32,512]{3,2,1,0:T(8,128)S(1)} %shard_map.43.t_ref, f32[8,1,32,512]{3,2,1,0:T(8,128)S(1)} %get-tuple-element.30.oylo, f32[8,1,32,512]{3,2,1,0:T(8,128)S(1)} %get-tuple-element.31.oyhi, f32[8,16,512]{2,1,0:T(8,128)S(1)} %get-tuple-element.32.ozlo, ...), custom_call_target="tpu_custom_call" | custom-call | tf_op jit(solution)/shard_map/pallas_call | solution.py:386
  77.4 1.6 %collective-permute-done.8 = f32[4,160,128]{2,1,0:T(8,128)S(1)} collective-permute-done((f32[4,160,128]{2,1,0:T(8,128)S(1)}, f32[4,160,128]{2,1,0:T(8,128)S(1)}, u32[]{:S(2)}, u32[]{:S(2)}) %collective-permute-start.8) | collective-permute-done | bytes 327712 | tf_op jit(solution)/shard_map/ppermute | solution.py:14
  79.0 5.5 %collective-permute-start.10 = (f32[160,128]{1,0:T(8,128)S(1)}, f32[160,128]{1,0:T(8,128)S(1)}, u32[]{:S(2)}, u32[]{:S(2)}) collective-permute-start(f32[160,128]{1,0:T(8,128)S(1)} %get-tuple-element.54), channel_id=1, source_target_pairs={{0,64},{1,65},{64,0},{65,1},{2,66},{3,67},{66,2},{67,3},{4,68},{5,... | collective-permute-start | bytes 245768 | tf_op jit(solution)/shard_map/ppermute | solution.py:14
  87.1 2.5 %collective-permute-done.11 = f32[160,128]{1,0:T(8,128)S(1)} collective-permute-done((f32[160,128]{1,0:T(8,128)S(1)}, f32[160,128]{1,0:T(8,128)S(1)}, u32[]{:S(2)}, u32[]{:S(2)}) %collective-permute-start.11) | collective-permute-done | bytes 81952 | tf_op jit(solution)/shard_map/ppermute | solution.py:14
  89.9 2.4 %collective-permute-start.12 = (f32[160,128]{1,0:T(8,128)S(1)}, f32[160,128]{1,0:T(8,128)S(1)}, u32[]{:S(2)}, u32[]{:S(2)}) collective-permute-start(f32[160,128]{1,0:T(8,128)S(1)} %fusion.1), channel_id=1, source_target_pairs={{0,2},{2,4},{4,6},{6,0},{1,3},{3,5},{5,7},{7,1},{8,10},{10,12},{12... | collective-permute-start | bytes 245768 | tf_op jit(solution)/shard_map/ppermute | solution.py:14
  92.3 3.3 %collective-permute-start.13 = (f32[160,128]{1,0:T(8,128)S(1)}, f32[160,128]{1,0:T(8,128)S(1)}, u32[]{:S(2)}, u32[]{:S(2)}) collective-permute-start(f32[160,128]{1,0:T(8,128)S(1)} %fusion.1), channel_id=1, source_target_pairs={{0,4},{2,6},{4,0},{6,2},{1,5},{3,7},{5,1},{7,3},{8,12},{10,14},{12... | collective-permute-start | bytes 245768 | tf_op jit(solution)/shard_map/ppermute | solution.py:14
  96.3 2.1 %collective-permute-done.13 = f32[160,128]{1,0:T(8,128)S(1)} collective-permute-done((f32[160,128]{1,0:T(8,128)S(1)}, f32[160,128]{1,0:T(8,128)S(1)}, u32[]{:S(2)}, u32[]{:S(2)}) %collective-permute-start.13) | collective-permute-done | bytes 81952 | tf_op jit(solution)/shard_map/ppermute | solution.py:14
  99.5 2.9 %collective-permute-start.15 = (f32[160,128]{1,0:T(8,128)S(1)}, f32[160,128]{1,0:T(8,128)S(1)}, u32[]{:S(2)}, u32[]{:S(2)}) collective-permute-start(f32[160,128]{1,0:T(8,128)S(1)} %add_add_fusion.1), channel_id=1, source_target_pairs={{0,8},{8,16},{16,24},{24,0},{1,9},{9,17},{17,25},{25,1},{2,10},{10... | collective-permute-start | bytes 245768 | tf_op jit(solution)/shard_map/ppermute | solution.py:14
  102.4 2.4 %collective-permute-start.16 = (f32[160,128]{1,0:T(8,128)S(1)}, f32[160,128]{1,0:T(8,128)S(1)}, u32[]{:S(2)}, u32[]{:S(2)}) collective-permute-start(f32[160,128]{1,0:T(8,128)S(1)} %add_add_fusion.1), channel_id=1, source_target_pairs={{0,16},{8,24},{16,0},{24,8},{1,17},{9,25},{17,1},{25,9},{2,18},{10... | collective-permute-start | bytes 245768 | tf_op jit(solution)/shard_map/ppermute | solution.py:14
  106.0 1.5 collective-permute-done.16
  109.2 4.2 %collective-permute-start.19 = (f32[160,128]{1,0:T(8,128)S(1)}, f32[160,128]{1,0:T(8,128)S(1)}, u32[]{:S(2)}, u32[]{:S(2)}) collective-permute-start(f32[160,128]{1,0:T(8,128)S(1)} %get-tuple-element.43), channel_id=1, source_target_pairs={{0,64},{1,65},{64,0},{65,1},{2,66},{3,67},{66,2},{67,3},{4,68},{5,... | collective-permute-start | bytes 245768 | tf_op jit(solution)/shard_map/ppermute | solution.py:14
  113.4 1.9 %collective-permute-start.20 = (f32[160,128]{1,0:T(8,128)S(1)}, f32[160,128]{1,0:T(8,128)S(1)}, u32[]{:S(2)}, u32[]{:S(2)}) collective-permute-start(f32[160,128]{1,0:T(8,128)S(1)} %get-tuple-element.43), channel_id=1, source_target_pairs={{0,65},{1,0},{64,1},{65,64},{2,67},{3,2},{66,3},{67,66},{4,69},{5,... | collective-permute-start | bytes 245768 | tf_op jit(solution)/shard_map/ppermute | solution.py:14
  116.8 3.9 %collective-permute-start.21 = (f32[4,160,128]{2,1,0:T(8,128)S(1)}, f32[4,160,128]{2,1,0:T(8,128)S(1)}, u32[]{:S(2)}, u32[]{:S(2)}) collective-permute-start(f32[4,160,128]{2,1,0:T(8,128)S(1)} %bitcast_dynamic-update-slice_fusion.2), channel_id=1, source_target_pairs={{0,32},{32,0},{1,33},{33,1},{2,34},{34,2},{3,35},{35,3},{4,36},{36... | collective-permute-start | bytes 983048 | tf_op jit(solution)/shard_map/ppermute | solution.py:14
  122.0 21.1 %shard_map.45 = (f32[512,512]{1,0:T(8,128)}, f32[512,512]{1,0:T(8,128)S(1)}) custom-call(f32[10,128,128]{2,1,0:T(8,128)S(1)} %bitcast.48), custom_call_target="tpu_custom_call" | custom-call | tf_op jit(solution)/shard_map/pallas_call | solution.py:133
  143.1 11.5 %shard_map.46 = f32[4096,512]{1,0:T(8,128)} custom-call(f32[4096,512]{1,0:T(8,128)} %bitcast.51, f32[512,512]{1,0:T(8,128)S(1)} %get-tuple-element.40.n_ref), custom_call_target="tpu_custom_call" | custom-call | tf_op jit(solution)/shard_map/pallas_call | solution.py:427
  (72 shorter events, 20.9 us)
Async XLA Ops:
  2.9 31.7 %collective-permute-start = (f32[9,1,32,512]{3,2,1,0:T(8,128)S(1)}, f32[9,1,32,512]{3,2,1,0:T(8,128)S(1)}, u32[]{:S(2)}, u32[]{:S(2)}) collective-permute-start(f32[9,1,32,512]{3,2,1,0:T(8,128)S(1)} %pad_maximum_fusion.1.yhi), channel_id=1, source_target_pairs={{0,32},{32,64},{64,96},{1,33},{33,65},{65,97},{2,34},{34,66},{66,9... | collective-permute-start | bytes 1769480 | tf_op jit(solution)/shard_map/ppermute | solution.py:450
  9.1 25.5 %collective-permute-start.1 = (f32[9,1,32,512]{3,2,1,0:T(8,128)S(1)}, f32[9,1,32,512]{3,2,1,0:T(8,128)S(1)}, u32[]{:S(2)}, u32[]{:S(2)}) collective-permute-start(f32[9,1,32,512]{3,2,1,0:T(8,128)S(1)} %pad_maximum_fusion.ylo), channel_id=1, source_target_pairs={{32,0},{64,32},{96,64},{33,1},{65,33},{97,65},{34,2},{66,34},{98,6... | collective-permute-start | bytes 1769480 | tf_op jit(solution)/shard_map/ppermute | solution.py:450
  15.0 19.6 %collective-permute-start.2 = (f32[9,16,512]{2,1,0:T(8,128)S(1)}, f32[9,16,512]{2,1,0:T(8,128)S(1)}, u32[]{:S(2)}, u32[]{:S(2)}) collective-permute-start(f32[9,16,512]{2,1,0:T(8,128)S(1)} %pad_maximum_fusion.3.zhi), channel_id=1, source_target_pairs={{0,1},{1,2},{2,3},{3,4},{4,5},{5,6},{6,7},{7,8},{8,9},{9,10},{10,1... | collective-permute-start | bytes 884744 | tf_op jit(solution)/shard_map/ppermute | solution.py:450
  17.4 17.2 %collective-permute-start.3 = (f32[9,16,512]{2,1,0:T(8,128)S(1)}, f32[9,16,512]{2,1,0:T(8,128)S(1)}, u32[]{:S(2)}, u32[]{:S(2)}) collective-permute-start(f32[9,16,512]{2,1,0:T(8,128)S(1)} %pad_maximum_fusion.2.zlo), channel_id=1, source_target_pairs={{1,0},{2,1},{3,2},{4,3},{5,4},{6,5},{7,6},{8,7},{9,8},{10,9},{11,1... | collective-permute-start | bytes 884744 | tf_op jit(solution)/shard_map/ppermute | solution.py:450
  37.5 27.3 %collective-permute-start.4 = (f32[8,1,32,512]{3,2,1,0:T(8,128)S(1)}, f32[8,1,32,512]{3,2,1,0:T(8,128)S(1)}, u32[]{:S(2)}, u32[]{:S(2)}) collective-permute-start(f32[8,1,32,512]{3,2,1,0:T(8,128)S(1)} %get-tuple-element.31.oyhi), channel_id=1, source_target_pairs={{0,32},{32,64},{64,96},{1,33},{33,65},{65,97},{2,34},{34,66},{66,9... | collective-permute-start | bytes 1572872 | tf_op jit(solution)/shard_map/ppermute | solution.py:450
  43.5 21.3 %collective-permute-start.5 = (f32[8,1,32,512]{3,2,1,0:T(8,128)S(1)}, f32[8,1,32,512]{3,2,1,0:T(8,128)S(1)}, u32[]{:S(2)}, u32[]{:S(2)}) collective-permute-start(f32[8,1,32,512]{3,2,1,0:T(8,128)S(1)} %get-tuple-element.30.oylo), channel_id=1, source_target_pairs={{32,0},{64,32},{96,64},{33,1},{65,33},{97,65},{34,2},{66,34},{98,6... | collective-permute-start | bytes 1572872 | tf_op jit(solution)/shard_map/ppermute | solution.py:450
  45.4 18.6 %collective-permute-start.6 = (f32[8,16,512]{2,1,0:T(8,128)S(1)}, f32[8,16,512]{2,1,0:T(8,128)S(1)}, u32[]{:S(2)}, u32[]{:S(2)}) collective-permute-start(f32[8,16,512]{2,1,0:T(8,128)S(1)} %get-tuple-element.33.ozhi), channel_id=1, source_target_pairs={{0,1},{1,2},{2,3},{3,4},{4,5},{5,6},{6,7},{7,8},{8,9},{9,10},{10,1... | collective-permute-start | bytes 786440 | tf_op jit(solution)/shard_map/ppermute | solution.py:450
  49.2 14.9 %collective-permute-start.7 = (f32[8,16,512]{2,1,0:T(8,128)S(1)}, f32[8,16,512]{2,1,0:T(8,128)S(1)}, u32[]{:S(2)}, u32[]{:S(2)}) collective-permute-start(f32[8,16,512]{2,1,0:T(8,128)S(1)} %get-tuple-element.32.ozlo), channel_id=1, source_target_pairs={{1,0},{2,1},{3,2},{4,3},{5,4},{6,5},{7,6},{8,7},{9,8},{10,9},{11,1... | collective-permute-start | bytes 786440 | tf_op jit(solution)/shard_map/ppermute | solution.py:450
  50.5 14.3 %copy-start.3 = (f32[32,512]{1,0:T(8,128)S(1)}, f32[32,512]{1,0:T(8,128)}, u32[]{:S(2)}) copy-start(f32[32,512]{1,0:T(8,128)} %copy-done.2) | copy-start | bytes 196612
  50.5 14.3 %copy-start.5 = (f32[32,512]{1,0:T(8,128)S(1)}, f32[32,512]{1,0:T(8,128)}, u32[]{:S(2)}) copy-start(f32[32,512]{1,0:T(8,128)} %copy-done.4) | copy-start | bytes 196612
  77.3 1.7 %collective-permute-start.8 = (f32[4,160,128]{2,1,0:T(8,128)S(1)}, f32[4,160,128]{2,1,0:T(8,128)S(1)}, u32[]{:S(2)}, u32[]{:S(2)}) collective-permute-start(f32[4,160,128]{2,1,0:T(8,128)S(1)} %dynamic-slice_bitcast_fusion), channel_id=1, source_target_pairs={{0,32},{32,0},{1,33},{33,1},{2,34},{34,2},{3,35},{35,3},{4,36},{36... | collective-permute-start | bytes 983048 | tf_op jit(solution)/shard_map/ppermute | solution.py:14
  79.0 8.0 %collective-permute-start.10 = (f32[160,128]{1,0:T(8,128)S(1)}, f32[160,128]{1,0:T(8,128)S(1)}, u32[]{:S(2)}, u32[]{:S(2)}) collective-permute-start(f32[160,128]{1,0:T(8,128)S(1)} %get-tuple-element.54), channel_id=1, source_target_pairs={{0,64},{1,65},{64,0},{65,1},{2,66},{3,67},{66,2},{67,3},{4,68},{5,... | collective-permute-start | bytes 245768 | tf_op jit(solution)/shard_map/ppermute | solution.py:14
  84.6 5.0 %collective-permute-start.11 = (f32[160,128]{1,0:T(8,128)S(1)}, f32[160,128]{1,0:T(8,128)S(1)}, u32[]{:S(2)}, u32[]{:S(2)}) collective-permute-start(f32[160,128]{1,0:T(8,128)S(1)} %get-tuple-element.53), channel_id=1, source_target_pairs={{0,65},{1,0},{64,1},{65,64},{2,67},{3,2},{66,3},{67,66},{4,69},{5,... | collective-permute-start | bytes 245768 | tf_op jit(solution)/shard_map/ppermute | solution.py:14
  85.4 4.5 %collective-permute-start.9 = (f32[160,128]{1,0:T(8,128)S(1)}, f32[160,128]{1,0:T(8,128)S(1)}, u32[]{:S(2)}, u32[]{:S(2)}) collective-permute-start(f32[160,128]{1,0:T(8,128)S(1)} %get-tuple-element.52), channel_id=1, source_target_pairs={{0,1},{1,64},{64,65},{65,0},{2,3},{3,66},{66,67},{67,2},{4,5},{5,6... | collective-permute-start | bytes 245768 | tf_op jit(solution)/shard_map/ppermute | solution.py:14
  89.9 6.4 %collective-permute-start.12 = (f32[160,128]{1,0:T(8,128)S(1)}, f32[160,128]{1,0:T(8,128)S(1)}, u32[]{:S(2)}, u32[]{:S(2)}) collective-permute-start(f32[160,128]{1,0:T(8,128)S(1)} %fusion.1), channel_id=1, source_target_pairs={{0,2},{2,4},{4,6},{6,0},{1,3},{3,5},{5,7},{7,1},{8,10},{10,12},{12... | collective-permute-start | bytes 245768 | tf_op jit(solution)/shard_map/ppermute | solution.py:14
  92.3 6.1 %collective-permute-start.13 = (f32[160,128]{1,0:T(8,128)S(1)}, f32[160,128]{1,0:T(8,128)S(1)}, u32[]{:S(2)}, u32[]{:S(2)}) collective-permute-start(f32[160,128]{1,0:T(8,128)S(1)} %fusion.1), channel_id=1, source_target_pairs={{0,4},{2,6},{4,0},{6,2},{1,5},{3,7},{5,1},{7,3},{8,12},{10,14},{12... | collective-permute-start | bytes 245768 | tf_op jit(solution)/shard_map/ppermute | solution.py:14
  95.6 3.9 %collective-permute-start.14 = (f32[160,128]{1,0:T(8,128)S(1)}, f32[160,128]{1,0:T(8,128)S(1)}, u32[]{:S(2)}, u32[]{:S(2)}) collective-permute-start(f32[160,128]{1,0:T(8,128)S(1)} %fusion.1), channel_id=1, source_target_pairs={{0,6},{2,0},{4,2},{6,4},{1,7},{3,1},{5,3},{7,5},{8,14},{10,8},{12,... | collective-permute-start | bytes 245768 | tf_op jit(solution)/shard_map/ppermute | solution.py:14
  99.5 6.5 %collective-permute-start.15 = (f32[160,128]{1,0:T(8,128)S(1)}, f32[160,128]{1,0:T(8,128)S(1)}, u32[]{:S(2)}, u32[]{:S(2)}) collective-permute-start(f32[160,128]{1,0:T(8,128)S(1)} %add_add_fusion.1), channel_id=1, source_target_pairs={{0,8},{8,16},{16,24},{24,0},{1,9},{9,17},{17,25},{25,1},{2,10},{10... | collective-permute-start | bytes 245768 | tf_op jit(solution)/shard_map/ppermute | solution.py:14
  102.4 5.1 %collective-permute-start.16 = (f32[160,128]{1,0:T(8,128)S(1)}, f32[160,128]{1,0:T(8,128)S(1)}, u32[]{:S(2)}, u32[]{:S(2)}) collective-permute-start(f32[160,128]{1,0:T(8,128)S(1)} %add_add_fusion.1), channel_id=1, source_target_pairs={{0,16},{8,24},{16,0},{24,8},{1,17},{9,25},{17,1},{25,9},{2,18},{10... | collective-permute-start | bytes 245768 | tf_op jit(solution)/shard_map/ppermute | solution.py:14
  104.9 3.6 %collective-permute-start.17 = (f32[160,128]{1,0:T(8,128)S(1)}, f32[160,128]{1,0:T(8,128)S(1)}, u32[]{:S(2)}, u32[]{:S(2)}) collective-permute-start(f32[160,128]{1,0:T(8,128)S(1)} %add_add_fusion.1), channel_id=1, source_target_pairs={{0,24},{8,0},{16,8},{24,16},{1,25},{9,1},{17,9},{25,17},{2,26},{10... | collective-permute-start | bytes 245768 | tf_op jit(solution)/shard_map/ppermute | solution.py:14
  108.5 6.8 %collective-permute-start.18 = (f32[160,128]{1,0:T(8,128)S(1)}, f32[160,128]{1,0:T(8,128)S(1)}, u32[]{:S(2)}, u32[]{:S(2)}) collective-permute-start(f32[160,128]{1,0:T(8,128)S(1)} %get-tuple-element.43), channel_id=1, source_target_pairs={{0,1},{1,64},{64,65},{65,0},{2,3},{3,66},{66,67},{67,2},{4,5},{5,6... | collective-permute-start | bytes 245768 | tf_op jit(solution)/shard_map/ppermute | solution.py:14
  109.2 6.7 %collective-permute-start.19 = (f32[160,128]{1,0:T(8,128)S(1)}, f32[160,128]{1,0:T(8,128)S(1)}, u32[]{:S(2)}, u32[]{:S(2)}) collective-permute-start(f32[160,128]{1,0:T(8,128)S(1)} %get-tuple-element.43), channel_id=1, source_target_pairs={{0,64},{1,65},{64,0},{65,1},{2,66},{3,67},{66,2},{67,3},{4,68},{5,... | collective-permute-start | bytes 245768 | tf_op jit(solution)/shard_map/ppermute | solution.py:14
  113.4 3.4 %collective-permute-start.20 = (f32[160,128]{1,0:T(8,128)S(1)}, f32[160,128]{1,0:T(8,128)S(1)}, u32[]{:S(2)}, u32[]{:S(2)}) collective-permute-start(f32[160,128]{1,0:T(8,128)S(1)} %get-tuple-element.43), channel_id=1, source_target_pairs={{0,65},{1,0},{64,1},{65,64},{2,67},{3,2},{66,3},{67,66},{4,69},{5,... | collective-permute-start | bytes 245768 | tf_op jit(solution)/shard_map/ppermute | solution.py:14
  116.8 5.1 %collective-permute-start.21 = (f32[4,160,128]{2,1,0:T(8,128)S(1)}, f32[4,160,128]{2,1,0:T(8,128)S(1)}, u32[]{:S(2)}, u32[]{:S(2)}) collective-permute-start(f32[4,160,128]{2,1,0:T(8,128)S(1)} %bitcast_dynamic-update-slice_fusion.2), channel_id=1, source_target_pairs={{0,32},{32,0},{1,33},{33,1},{2,34},{34,2},{3,35},{35,3},{4,36},{36... | collective-permute-start | bytes 983048 | tf_op jit(solution)/shard_map/ppermute | solution.py:14
  (8 other events, 32.6 us)

commit v2 on v1

--- a/solution.py
+++ b/solution.py
@@ -178,12 +178,16 @@
     return jnp.concatenate([a[: n - 8], end], 0)
 
 
-def relax_slabs(u, wx, wy, wz, emit):
+def flow_both(u, w, wb):
+    return w * (ahead(u, 1) - u) + wb * (behind(u, 1) - u)
+
+
+def relax_slabs(u, wx, wxb, wy, wz, emit):
     count = wx.shape[0]
     below = None
     for y in range(count):
         c = u(y)
-        t = flow_along(c, wx[y], 1) + flow_along(c, wz[y], 0)
+        t = flow_both(c, wx[y], wxb[y]) + flow_along(c, wz[y], 0)
         if below is not None:
             t = t - below
         if y + 1 < count:
@@ -192,28 +196,9 @@
         emit(y, c, t)
 
 
-def own_kernel(f_ref, k_ref, p_ref, wx, wy, wz, pylo, pyhi, pzlo, pzhi):
-    count, nz, _ = k_ref.shape
-
-    @pl.when(pl.program_id(0) == 0)
-    def _():
-        for y in range(count):
-            k = k_ref[y]
-            wx[y] = link_along(k, 1)
-            wz[y] = link_along(k, 0)
-            wy[y] = link(k, k_ref[y + 1]) if y + 1 < count else jnp.zeros_like(k)
-
-    def emit(y, c, t):
-        r = c + t
-        p_ref[0, y] = r
-        if y == 0:
-            pylo[0, 0] = r
-        if y == count - 1:
-            pyhi[0, 0] = r
-        pzlo[0, y : y + 1] = r[0:1]
-        pzhi[0, y : y + 1] = r[nz - 1 : nz]
-
-    relax_slabs(lambda y: f_ref[0, y], wx, wy, wz, emit)
+DEPTH = 4
+FAR = pl.BlockSpec(memory_space=pltpu.HBM)
+NEAR = pl.BlockSpec(memory_space=pltpu.VMEM)
 
 
 def far(x):
@@ -224,22 +209,97 @@
     return pltpu.CompilerParams(vmem_limit_bytes=mib * 2**20)
 
 
+def stream(count, fetch, work, store):
+    if fetch is not None:
+        for i in range(min(DEPTH, count)):
+            fetch(i).start()
+
+    def step(i, carry):
+        if fetch is not None:
+            fetch(i).wait()
+
+            @pl.when(i + DEPTH < count)
+            def _():
+                fetch(i + DEPTH).start()
+
+        work(i)
+        if store is not None:
+            store(i).start()
+        return carry
+
+    lax.fori_loop(0, count, step, 0)
+
+
+def drain(count, store):
+    for i in range(count):
+        store(i).wait()
+
+
+def own_kernel(
+    f_far, k_far, p_far, wx_far, wy_far, wz_far, pylo, pyhi, pzlo, pzhi,
+    fbuf, k_ref, pbuf, wx, wxb, wy, wz, f_sem, p_sem, k_sem, w_sem,
+):
+    nf, count, nz, _ = fbuf.shape
+    k_copy = pltpu.make_async_copy(k_far, k_ref, k_sem)
+    k_copy.start()
+    w_copies = [
+        pltpu.make_async_copy(a, b, w_sem.at[i])
+        for i, (a, b) in enumerate(((wx, wx_far), (wy, wy_far), (wz, wz_far)))
+    ]
+
+    def fetch(f):
+        return pltpu.make_async_copy(f_far.at[f], fbuf.at[f], f_sem.at[f])
+
+    def store(f):
+        return pltpu.make_async_copy(pbuf.at[f], p_far.at[f], p_sem.at[f])
+
+    def work(f):
+        @pl.when(f == 0)
+        def _():
+            k_copy.wait()
+            for y in range(count):
+                k = k_ref[y]
+                w = link_along(k, 1)
+                wx[y] = w
+                wxb[y] = behind(w, 1)
+                wz[y] = link_along(k, 0)
+                wy[y] = link(k, k_ref[y + 1]) if y + 1 < count else jnp.zeros_like(k)
+            for c in w_copies:
+                c.start()
+
+        def emit(y, c, t):
+            r = c + t
+            pbuf[f, y] = r
+            if y == 0:
+                pylo[f, 0] = r
+            if y == count - 1:
+                pyhi[f, 0] = r
+            pzlo[f, y : y + 1] = r[0:1]
+            pzhi[f, y : y + 1] = r[nz - 1 : nz]
+
+        relax_slabs(lambda y: fbuf[f, y], wx, wxb, wy, wz, emit)
+
+    stream(nf, fetch, work, store)
+    drain(nf, store)
+    for c in w_copies:
+        c.wait()
+
+
 def own_relax(fields, conductance):
     nf, ny, nz, nx = fields.shape
-    block = pl.BlockSpec((1, ny, nz, nx), lambda f: (f, 0, 0, 0))
-    whole = pl.BlockSpec((ny, nz, nx), lambda f: (0, 0, 0))
-    zface = pl.BlockSpec((1, ny, nx), lambda f: (f, 0, 0))
     w = pltpu.HBM((ny, nz, nx), jnp.float32)
     yf = jax.ShapeDtypeStruct((nf, 1, nz, nx), jnp.float32)
-    yface = pl.BlockSpec((1, 1, nz, nx), lambda f: (f, 0, 0, 0))
     zf = jax.ShapeDtypeStruct((nf, ny, nx), jnp.float32)
+    big = pltpu.VMEM(fields.shape, jnp.float32)
+    one = pltpu.VMEM((ny, nz, nx), jnp.float32)
+    sem = pltpu.SemaphoreType.DMA
     return pl.pallas_call(
         own_kernel,
-        grid=(nf,),
-        in_specs=[block, whole],
-        out_specs=(block, whole, whole, whole, yface, yface, zface, zface),
+        in_specs=[FAR, FAR],
+        out_specs=(FAR,) * 4 + (NEAR,) * 4,
         out_shape=(pltpu.HBM(fields.shape, jnp.float32), w, w, w, yf, yf, zf, zf),
-        compiler_params=limit(24),
+        scratch_shapes=[big, one, big, one, one, one, one, sem((nf,)), sem((nf,)), sem, sem((3,))],
+        compiler_params=limit(32),
     )(far(fields), far(conductance))
 
 
@@ -287,152 +347,179 @@
     )(*args)
 
 
-def again_kernel(p_ref, wx, wy, wz, oylo, oyhi, ozlo, ozhi, t_ref, once):
-    ny, nz, _ = wx.shape
-    for y in range(ny):
-        if y == 0:
-            once[y] = oylo[0, 0]
-        elif y == ny - 1:
-            once[y] = oyhi[0, 0]
-        else:
-            once[y] = p_ref[0, y]
-            once[y, 0:1] = ozlo[0, y : y + 1]
-            once[y, nz - 1 : nz] = ozhi[0, y : y + 1]
-
-    def emit(y, c, t):
-        t_ref[0, y] = c + t
-
-    relax_slabs(lambda y: once[y], wx, wy, wz, emit)
-
-
-def specs(nf, ny, nz, nx):
-    block = pl.BlockSpec((1, ny, nz, nx), lambda f: (f, 0, 0, 0))
-    yface = pl.BlockSpec((1, 1, nz, nx), lambda f: (f, 0, 0, 0))
-    zface = pl.BlockSpec((1, ny, nx), lambda f: (f, 0, 0))
-    return block, yface, zface
+def again_kernel(
+    p_far, wx_far, wy_far, wz_far, oylo, oyhi, ozlo, ozhi, t_ref, once, wx, wxb, wy, wz, p_sem, w_sem
+):
+    nf, ny, nz, _ = once.shape
+    w_copies = [
+        pltpu.make_async_copy(a, b, w_sem.at[i])
+        for i, (a, b) in enumerate(((wx_far, wx), (wy_far, wy), (wz_far, wz)))
+    ]
+    for c in w_copies:
+        c.start()
+
+    def fetch(f):
+        return pltpu.make_async_copy(p_far.at[f], once.at[f], p_sem.at[f])
+
+    def work(f):
+        @pl.when(f == 0)
+        def _():
+            for c in w_copies:
+                c.wait()
+            for y in range(ny):
+                wxb[y] = behind(wx[y], 1)
+
+        once[f, 0] = oylo[f, 0]
+        once[f, ny - 1] = oyhi[f, 0]
+        for y in range(1, ny - 1):
+            once[f, y, 0:1] = ozlo[f, y : y + 1]
+            once[f, y, nz - 1 : nz] = ozhi[f, y : y + 1]
+
+        def emit(y, c, t):
+            t_ref[f, y] = c + t
+
+        relax_slabs(lambda y: once[f, y], wx, wxb, wy, wz, emit)
+
+    stream(nf, fetch, work, None)
 
 
 def again_relax(p, wx, wy, wz, *faces):
     nf, ny, nz, nx = p.shape
-    block, yface, zface = specs(*p.shape)
-    whole = pl.BlockSpec((ny, nz, nx), lambda f: (0, 0, 0))
+    one = pltpu.VMEM((ny, nz, nx), jnp.float32)
+    sem = pltpu.SemaphoreType.DMA
     return pl.pallas_call(
         again_kernel,
-        grid=(nf,),
-        in_specs=[block, whole, whole, whole, yface, yface, zface, zface],
-        out_specs=block,
+        in_specs=[FAR] * 4 + [NEAR] * 4,
+        out_specs=NEAR,
         out_shape=jax.ShapeDtypeStruct(p.shape, jnp.float32),
-        scratch_shapes=[pltpu.VMEM((ny, nz, nx), jnp.float32)],
-        compiler_params=limit(24),
+        scratch_shapes=[pltpu.VMEM(p.shape, jnp.float32), one, one, one, one, sem((nf,)), sem((3,))],
+        compiler_params=limit(32),
     )(far(p), far(wx), far(wy), far(wz), *faces)
 
 
 def edge_kernel(
     t_ref, oylo, oyhi, ozlo, ozhi, yu, yd, zl, zr, lyu, lyd, lzl, lzr,
-    r_ref, g_ref, high, low,
+    r_far, g_ref, rbuf, high, low, r_sem,
 ):
-    f = pl.program_id(0)
-    _, ny, nz, nx = t_ref.shape
-    left = lzl[...] * (zl[0] - ozlo[0])
-    right = lzr[...] * (zr[0] - ozhi[0])
-    for y in range(ny):
-        r = t_ref[0, y]
-        if y == 0:
-            r = r + lyu[...] * (yu[0, 0] - oylo[0, 0])
-        if y == ny - 1:
-            r = r + lyd[...] * (yd[0, 0] - oyhi[0, 0])
-        r = add_first_row(r, left[y : y + 1])
-        r = add_last_row(r, right[y : y + 1])
-        r_ref[0, y] = r
-        h = r.astype(jnp.bfloat16)
-        at = pl.ds(pl.multiple_of(f * (ny * nz) + y * nz, nz), nz)
-        high[at] = h
-        low[at] = (r - h.astype(jnp.float32)).astype(jnp.bfloat16)
+    nf, ny, nz, nx = t_ref.shape
+
+    def store(f):
+        return pltpu.make_async_copy(rbuf.at[f], r_far.at[f], r_sem.at[f])
+
+    def work(f):
+        left = lzl[...] * (zl[f] - ozlo[f])
+        right = lzr[...] * (zr[f] - ozhi[f])
+        for y in range(ny):
+            r = t_ref[f, y]
+            if y == 0:
+                r = r + lyu[...] * (yu[f, 0] - oylo[f, 0])
+            if y == ny - 1:
+                r = r + lyd[...] * (yd[f, 0] - oyhi[f, 0])
+            r = add_first_row(r, left[y : y + 1])
+            r = add_last_row(r, right[y : y + 1])
+            rbuf[f, y] = r
+            h = r.astype(jnp.bfloat16)
+            at = pl.ds(pl.multiple_of(f * (ny * nz) + y * nz, nz), nz)
+            high[at] = h
+            low[at] = (r - h.astype(jnp.float32)).astype(jnp.bfloat16)
+
+    stream(nf, None, work, store)
 
     def cross(a, b):
         return lax.dot_general(a, b, (((0,), (0,)), ((), ())), preferred_element_type=jnp.float32)
 
-    @pl.when(f == pl.num_programs(0) - 1)
-    def _():
-        half = nx // 2
-        part = (slice(0, half), slice(half, nx))
-        acc_hh, acc_hl = [], []
-        for i in range(3):
-            a, b = part[i // 2], part[(i + 1) // 2]
-            acc_hh.append(cross(high[:, a], high[:, b]) + cross(low[:, a], low[:, b]))
-        for i in range(4):
-            acc_hl.append(cross(high[:, part[i // 2]], low[:, part[i % 2]]))
-        per = half // BLK
-
-        def inner_block(i, j):
-            return slice(i % per * BLK, (i % per + 1) * BLK), slice(j % per * BLK, (j % per + 1) * BLK)
-
-        t = 0
-        for i in range(2 * per):
-            for j in range(i, 2 * per):
-                p, q = i // per, j // per
-                a, b = inner_block(i, j)
-                g_ref[t] = acc_hh[p + q][a, b] + acc_hl[2 * p + q][a, b] + acc_hl[2 * q + p][b, a].T
-                t += 1
+    half = nx // 2
+    part = (slice(0, half), slice(half, nx))
+    acc_hh, acc_hl = [], []
+    for i in range(3):
+        a, b = part[i // 2], part[(i + 1) // 2]
+        acc_hh.append(cross(high[:, a], high[:, b]) + cross(low[:, a], low[:, b]))
+    for i in range(4):
+        acc_hl.append(cross(high[:, part[i // 2]], low[:, part[i % 2]]))
+    per = half // BLK
+
+    def inner_block(i, j):
+        return slice(i % per * BLK, (i % per + 1) * BLK), slice(j % per * BLK, (j % per + 1) * BLK)
+
+    t = 0
+    for i in range(2 * per):
+        for j in range(i, 2 * per):
+            p, q = i // per, j // per
+            a, b = inner_block(i, j)
+            g_ref[t] = acc_hh[p + q][a, b] + acc_hl[2 * p + q][a, b] + acc_hl[2 * q + p][b, a].T
+            t += 1
+
+    drain(nf, store)
 
 
 def edge_relax(t, faces, halos, links):
     nf, ny, nz, nx = t.shape
-    block, yface, zface = specs(*t.shape)
-    ly = pl.BlockSpec((nz, nx), lambda f: (0, 0))
-    lz = pl.BlockSpec((ny, nx), lambda f: (0, 0))
     cnt = nx // BLK
     nb = cnt * (cnt + 1) // 2
     return pl.pallas_call(
         edge_kernel,
-        grid=(nf,),
-        in_specs=[block] + [yface, yface, zface, zface] * 2 + [ly, ly, lz, lz],
-        out_specs=(block, pl.BlockSpec((nb, BLK, BLK), lambda f: (0, 0, 0))),
+        in_specs=[NEAR] * 13,
+        out_specs=(FAR, NEAR),
         out_shape=(
             pltpu.HBM(t.shape, jnp.float32),
             jax.ShapeDtypeStruct((nb, BLK, BLK), jnp.float32),
         ),
-        scratch_shapes=[pltpu.VMEM((nf * ny * nz, nx), jnp.bfloat16)] * 2,
-        compiler_params=limit(24),
+        scratch_shapes=[pltpu.VMEM(t.shape, jnp.float32)]
+        + [pltpu.VMEM((nf * ny * nz, nx), jnp.bfloat16)] * 2
+        + [pltpu.SemaphoreType.DMA((nf,))],
+        compiler_params=limit(32),
     )(t, *faces, *halos, *links)
 
 
-def basis_kernel(r_ref, n_ref, o_ref, high, low):
-    @pl.when(pl.program_id(0) == 0)
-    def _():
-        n = n_ref[...]
-        h = n.astype(jnp.bfloat16)
-        high[...] = h
-        low[...] = (n - h.astype(jnp.float32)).astype(jnp.bfloat16)
-
-    r = r_ref[...]
-    a = r.astype(jnp.bfloat16)
-    b = (r - a.astype(jnp.float32)).astype(jnp.bfloat16)
-    width = r.shape[1]
+def basis_kernel(r_far, n_ref, o_far, rbuf, obuf, high, low, r_sem, o_sem):
+    count, chunk, width = rbuf.shape
     step = 256
-    for lo in range(0, width, step):
-        hi = lo + step
-
-        def times(x, m):
-            return lax.dot_general(
-                x[:, 0:hi], m[lo:hi, 0:hi], (((1,), (1,)), ((), ())), preferred_element_type=jnp.float32
-            )
-
-        o_ref[:, lo:hi] = times(a, high) + (times(a, low) + times(b, high))
+
+    def fetch(i):
+        return pltpu.make_async_copy(r_far.at[i], rbuf.at[i], r_sem.at[i])
+
+    def store(i):
+        return pltpu.make_async_copy(obuf.at[i], o_far.at[i], o_sem.at[i])
+
+    def work(i):
+        @pl.when(i == 0)
+        def _():
+            n = n_ref[...]
+            h = n.astype(jnp.bfloat16)
+            high[...] = h
+            low[...] = (n - h.astype(jnp.float32)).astype(jnp.bfloat16)
+
+        r = rbuf[i]
+        a = r.astype(jnp.bfloat16)
+        b = (r - a.astype(jnp.float32)).astype(jnp.bfloat16)
+        for lo in range(0, width, step):
+            hi = lo + step
+
+            def times(x, m):
+                return lax.dot_general(
+                    x[:, 0:hi], m[lo:hi, 0:hi], (((1,), (1,)), ((), ())), preferred_element_type=jnp.float32
+                )
+
+            obuf[i, :, lo:hi] = times(a, high) + (times(a, low) + times(b, high))
+
+    stream(count, fetch, work, store)
+    drain(count, store)
 
 
 def basis_of(rows, inverse_t, chunk=512):
     m, nx = rows.shape
-    block = pl.BlockSpec((chunk, nx), lambda i: (i, 0))
+    cut = (m // chunk, chunk, nx)
+    big = pltpu.VMEM(cut, jnp.float32)
+    sem = pltpu.SemaphoreType.DMA((m // chunk,))
     return pl.pallas_call(
         basis_kernel,
-        grid=(m // chunk,),
-        in_specs=[block, pl.BlockSpec((nx, nx), lambda i: (0, 0))],
-        out_specs=block,
-        out_shape=jax.ShapeDtypeStruct((m, nx), jnp.float32),
-        scratch_shapes=[pltpu.VMEM((nx, nx), jnp.bfloat16)] * 2,
-        compiler_params=pltpu.CompilerParams(vmem_limit_bytes=24 * 2**20),
-    )(far(rows), inverse_t)
+        in_specs=[FAR, NEAR],
+        out_specs=FAR,
+        out_shape=pltpu.HBM(cut, jnp.float32),
+        scratch_shapes=[big, big] + [pltpu.VMEM((nx, nx), jnp.bfloat16)] * 2 + [sem, sem],
+        compiler_params=limit(32),
+    )(far(rows.reshape(cut)), inverse_t)
+
 
 BY = ("yh", "c")
 BZ = ("x", "z", "yl")

time: 156 us -> 142 us (0.910)
  Pallas kernels: 73.9 us -> 59.9 us
  waiting for transfers between devices: 13.7 us -> 15.3 us
    pallas_call x4, Pallas kernels: 52.4 us -> 38.4 us  [the longest x1 11.4 us: own_relax(): pl.pallas_call(own_kernel, in_specs=[FAR, FAR], out_specs=(FAR,) * 4 + (N...]
    ppermute x8, waiting for transfers between devices: 0.02 us -> 2.91 us  [from_next(): lax.ppermute(piece, axes, [(i + step, i) for i in range(n) if 0 <= i + st...]
    ppermute x14, starting transfers between devices: 30.6 us -> 28.5 us  [shifted(): lax.ppermute(piece, axes, [(i, (i + distance) % count) for i in range(cou...]
  transfers between devices with their start and end apart: 22 -> 22, of which waited for: 11 -> 13; matrix products, arithmetic and copies ran while one was open for 3% -> 3% of each run, Pallas kernels for 19% -> 15%
where the time goes in v2:
time: 142 us; the launch traced here: 141 us
  Pallas kernels  59.9 us (42%)
  starting transfers between devices  54.3 us (38%)
  waiting for transfers between devices  15.3 us (11%)
  local copies, waits for them, and re-layouts  10.4 us (7%)
    ppermute x14, starting transfers between devices, shifted(): lax.ppermute(piece, axes, [(i, (i + distance) % count) for i in range(cou...  28.5 us
    ppermute x8, starting transfers between devices, from_next(): lax.ppermute(piece, axes, [(i + step, i) for i in range(n) if 0 <= i + st...  25.9 us
    pallas_call x1, Pallas kernels, factor_and_inverse(): pl.pallas_call(factor_kernel, out_shape=(square, square), in_specs=[whole...  21.2 us
    ppermute x14, waiting for transfers between devices, shifted(): lax.ppermute(piece, axes, [(i, (i + distance) % count) for i in range(cou...  12.4 us
    pallas_call x1, Pallas kernels, own_relax(): pl.pallas_call(own_kernel, in_specs=[FAR, FAR], out_specs=(FAR,) * 4 + (N...  11.4 us
    pallas_call x1, Pallas kernels, again_relax(): pl.pallas_call(again_kernel, in_specs=[FAR] * 4 + [NEAR] * 4, out_specs=N...  9.71 us
    pallas_call x1, Pallas kernels, basis_of(): pl.pallas_call(basis_kernel, in_specs=[FAR, NEAR], out_specs=FAR, out_sha...  9.07 us
    pallas_call x1, Pallas kernels, edge_relax(): pl.pallas_call(edge_kernel, in_specs=[NEAR] * 13, out_specs=(FAR, NEAR),...  8.14 us
  transfers between devices with their start and end apart: 22, of which 13 were waited for; matrix products, arithmetic and copies ran while one was open for 3% of the time, Pallas kernels for 15%

profile of v2, /device:TPU:1, one launch (start us, length us, event | category | flops | bytes accessed | tf_op | source)
XLA Modules:
  0.0 141.4 jit_solution(15115440407073909862)
XLA Ops:
  2.9 6.2 %collective-permute-start = (f32[9,1,32,512]{3,2,1,0:T(8,128)S(1)}, f32[9,1,32,512]{3,2,1,0:T(8,128)S(1)}, u32[]{:S(2)}, u32[]{:S(2)}) collective-permute-start(f32[9,1,32,512]{3,2,1,0:T(8,128)S(1)} %pad_maximum_fusion.1.yhi), channel_id=1, source_target_pairs={{0,32},{32,64},{64,96},{1,33},{33,65},{65,97},{2,34},{34,66},{66,9... | collective-permute-start | bytes 1769480 | tf_op jit(solution)/shard_map/ppermute | solution.py:537
  9.1 1.9 %collective-permute-start.1 = (f32[9,1,32,512]{3,2,1,0:T(8,128)S(1)}, f32[9,1,32,512]{3,2,1,0:T(8,128)S(1)}, u32[]{:S(2)}, u32[]{:S(2)}) collective-permute-start(f32[9,1,32,512]{3,2,1,0:T(8,128)S(1)} %pad_maximum_fusion.ylo), channel_id=1, source_target_pairs={{32,0},{64,32},{96,64},{33,1},{65,33},{97,65},{34,2},{66,34},{98,6... | collective-permute-start | bytes 1769480 | tf_op jit(solution)/shard_map/ppermute | solution.py:537
  11.1 2.8 %fusion.2 = (f32[8,16,1,512]{3,2,1,0:T(1,128)S(1)}, f32[8,16,1,512]{3,2,1,0:T(1,128)S(1)}) fusion(f32[8,16,32,512]{3,2,1,0:T(8,128)} %f_far.1), kind=kLoop, calls=%fused_computation.27 | loop fusion | bytes 1048576 | tf_op jit(solution)/shard_map/slice | solution.py:544
  15.0 2.3 %collective-permute-start.2 = (f32[9,16,512]{2,1,0:T(8,128)S(1)}, f32[9,16,512]{2,1,0:T(8,128)S(1)}, u32[]{:S(2)}, u32[]{:S(2)}) collective-permute-start(f32[9,16,512]{2,1,0:T(8,128)S(1)} %pad_maximum_fusion.3.zhi), channel_id=1, source_target_pairs={{0,1},{1,2},{2,3},{3,4},{4,5},{5,6},{6,7},{7,8},{8,9},{9,10},{10,1... | collective-permute-start | bytes 884744 | tf_op jit(solution)/shard_map/ppermute | solution.py:537
  18.7 11.4 %shard_map.41 = (f32[8,16,32,512]{3,2,1,0:T(8,128)}, f32[16,32,512]{2,1,0:T(8,128)}, f32[16,32,512]{2,1,0:T(8,128)}, f32[16,32,512]{2,1,0:T(8,128)}, f32[8,1,32,...) custom-call(f32[8,16,32,512]{3,2,1,0:T(8,128)} %f_far.1, ...), custom_call_target="tpu_custom_call" | custom-call | tf_op jit(solution)/shard_map/pallas_call | solution.py:296
  33.0 7.8 %collective-permute-start.4 = (f32[8,1,32,512]{3,2,1,0:T(8,128)S(1)}, f32[8,1,32,512]{3,2,1,0:T(8,128)S(1)}, u32[]{:S(2)}, u32[]{:S(2)}) collective-permute-start(f32[8,1,32,512]{3,2,1,0:T(8,128)S(1)} %get-tuple-element.31.oyhi), channel_id=1, source_target_pairs={{0,32},{32,64},{64,96},{1,33},{33,65},{65,97},{2,34},{34,66},{66,9... | collective-permute-start | bytes 1572872 | tf_op jit(solution)/shard_map/ppermute | solution.py:537
  40.8 1.9 %collective-permute-start.5 = (f32[8,1,32,512]{3,2,1,0:T(8,128)S(1)}, f32[8,1,32,512]{3,2,1,0:T(8,128)S(1)}, u32[]{:S(2)}, u32[]{:S(2)}) collective-permute-start(f32[8,1,32,512]{3,2,1,0:T(8,128)S(1)} %get-tuple-element.30.oylo), channel_id=1, source_target_pairs={{32,0},{64,32},{96,64},{33,1},{65,33},{97,65},{34,2},{66,34},{98,6... | collective-permute-start | bytes 1572872 | tf_op jit(solution)/shard_map/ppermute | solution.py:537
  42.8 3.1 %collective-permute-start.6 = (f32[8,16,512]{2,1,0:T(8,128)S(1)}, f32[8,16,512]{2,1,0:T(8,128)S(1)}, u32[]{:S(2)}, u32[]{:S(2)}) collective-permute-start(f32[8,16,512]{2,1,0:T(8,128)S(1)} %get-tuple-element.33.ozhi), channel_id=1, source_target_pairs={{0,1},{1,2},{2,3},{3,4},{4,5},{5,6},{6,7},{7,8},{8,9},{9,10},{10,1... | collective-permute-start | bytes 786440 | tf_op jit(solution)/shard_map/ppermute | solution.py:537
  47.3 9.7 %shard_map.43.t_ref = f32[8,16,32,512]{3,2,1,0:T(8,128)S(1)} custom-call(f32[8,16,32,512]{3,2,1,0:T(8,128)} %get-tuple-element.22.p_far, f32[16,32,512]{2,1,0:T(8,128)} %get-tuple-element.23.wx_far, f32[16,32,512]{2,1,0:T(8,128)} %get-tuple-element.24.wy_far, f32[16,32,512]{2,1,0:T(8,128)} %get-tuple-element.25.wz_far, ...), custom_call_target="tpu_custom_call" | custom-call | tf_op jit(solution)/shard_map/pallas_call | solution.py:390
  58.2 1.7 %collective-permute-done.7.zr = f32[8,16,512]{2,1,0:T(8,128)S(1)} collective-permute-done((f32[8,16,512]{2,1,0:T(8,128)S(1)}, f32[8,16,512]{2,1,0:T(8,128)S(1)}, u32[]{:S(2)}, u32[]{:S(2)}) %collective-permute-start.7) | collective-permute-done | bytes 262176 | tf_op jit(solution)/shard_map/ppermute | solution.py:537
  61.5 8.1 %shard_map.44 = (f32[8,16,32,512]{3,2,1,0:T(8,128)}, f32[10,128,128]{2,1,0:T(8,128)S(1)}) custom-call(f32[8,16,32,512]{3,2,1,0:T(8,128)S(1)} %shard_map.43.t_ref, f32[8,1,32,512]{3,2,1,0:T(8,128)S(1)} %get-tuple-element.30.oylo, f32[8,1,32,512]{3,2,1,0:T(8,128)S(1)} %get-tuple-element.31.oyhi, f32[8,16,512]{2,1,0:T(8,128)S(1)} %get-tuple-element.32.ozlo, ...), custom_call_target="tpu_custom_call" | custom-call | tf_op jit(solution)/shard_map/pallas_call | solution.py:459
  69.8 1.6 %collective-permute-done.8 = f32[4,160,128]{2,1,0:T(8,128)S(1)} collective-permute-done((f32[4,160,128]{2,1,0:T(8,128)S(1)}, f32[4,160,128]{2,1,0:T(8,128)S(1)}, u32[]{:S(2)}, u32[]{:S(2)}) %collective-permute-start.8) | collective-permute-done | bytes 327712 | tf_op jit(solution)/shard_map/ppermute | solution.py:14
  71.5 6.5 %collective-permute-start.10 = (f32[160,128]{1,0:T(8,128)S(1)}, f32[160,128]{1,0:T(8,128)S(1)}, u32[]{:S(2)}, u32[]{:S(2)}) collective-permute-start(f32[160,128]{1,0:T(8,128)S(1)} %get-tuple-element.54), channel_id=1, source_target_pairs={{0,64},{1,65},{64,0},{65,1},{2,66},{3,67},{66,2},{67,3},{4,68},{5,... | collective-permute-start | bytes 245768 | tf_op jit(solution)/shard_map/ppermute | solution.py:14
  80.5 2.2 %collective-permute-done.11 = f32[160,128]{1,0:T(8,128)S(1)} collective-permute-done((f32[160,128]{1,0:T(8,128)S(1)}, f32[160,128]{1,0:T(8,128)S(1)}, u32[]{:S(2)}, u32[]{:S(2)}) %collective-permute-start.11) | collective-permute-done | bytes 81952 | tf_op jit(solution)/shard_map/ppermute | solution.py:14
  84.3 1.6 %collective-permute-start.13 = (f32[160,128]{1,0:T(8,128)S(1)}, f32[160,128]{1,0:T(8,128)S(1)}, u32[]{:S(2)}, u32[]{:S(2)}) collective-permute-start(f32[160,128]{1,0:T(8,128)S(1)} %fusion.1), channel_id=1, source_target_pairs={{0,4},{2,6},{4,0},{6,2},{1,5},{3,7},{5,1},{7,3},{8,12},{10,14},{12... | collective-permute-start | bytes 245768 | tf_op jit(solution)/shard_map/ppermute | solution.py:14
  85.9 2.0 %collective-permute-start.14 = (f32[160,128]{1,0:T(8,128)S(1)}, f32[160,128]{1,0:T(8,128)S(1)}, u32[]{:S(2)}, u32[]{:S(2)}) collective-permute-start(f32[160,128]{1,0:T(8,128)S(1)} %fusion.1), channel_id=1, source_target_pairs={{0,6},{2,0},{4,2},{6,4},{1,7},{3,1},{5,3},{7,5},{8,14},{10,8},{12,... | collective-permute-start | bytes 245768 | tf_op jit(solution)/shard_map/ppermute | solution.py:14
  87.9 1.6 %collective-permute-done.13 = f32[160,128]{1,0:T(8,128)S(1)} collective-permute-done((f32[160,128]{1,0:T(8,128)S(1)}, f32[160,128]{1,0:T(8,128)S(1)}, u32[]{:S(2)}, u32[]{:S(2)}) %collective-permute-start.13) | collective-permute-done | bytes 81952 | tf_op jit(solution)/shard_map/ppermute | solution.py:14
  91.1 2.5 %collective-permute-start.16 = (f32[160,128]{1,0:T(8,128)S(1)}, f32[160,128]{1,0:T(8,128)S(1)}, u32[]{:S(2)}, u32[]{:S(2)}) collective-permute-start(f32[160,128]{1,0:T(8,128)S(1)} %add_add_fusion.1), channel_id=1, source_target_pairs={{0,16},{8,24},{16,0},{24,8},{1,17},{9,25},{17,1},{25,9},{2,18},{10... | collective-permute-start | bytes 245768 | tf_op jit(solution)/shard_map/ppermute | solution.py:14
  94.8 1.5 %collective-permute-done.16 = f32[160,128]{1,0:T(8,128)S(1)} collective-permute-done((f32[160,128]{1,0:T(8,128)S(1)}, f32[160,128]{1,0:T(8,128)S(1)}, u32[]{:S(2)}, u32[]{:S(2)}) %collective-permute-start.16) | collective-permute-done | bytes 81952 | tf_op jit(solution)/shard_map/ppermute | solution.py:14
  97.9 4.2 %collective-permute-start.19 = (f32[160,128]{1,0:T(8,128)S(1)}, f32[160,128]{1,0:T(8,128)S(1)}, u32[]{:S(2)}, u32[]{:S(2)}) collective-permute-start(f32[160,128]{1,0:T(8,128)S(1)} %get-tuple-element.43), channel_id=1, source_target_pairs={{0,64},{1,65},{64,0},{65,1},{2,66},{3,67},{66,2},{67,3},{4,68},{5,... | collective-permute-start | bytes 245768 | tf_op jit(solution)/shard_map/ppermute | solution.py:14
  102.1 1.9 %collective-permute-start.20 = (f32[160,128]{1,0:T(8,128)S(1)}, f32[160,128]{1,0:T(8,128)S(1)}, u32[]{:S(2)}, u32[]{:S(2)}) collective-permute-start(f32[160,128]{1,0:T(8,128)S(1)} %get-tuple-element.43), channel_id=1, source_target_pairs={{0,65},{1,0},{64,1},{65,64},{2,67},{3,2},{66,3},{67,66},{4,69},{5,... | collective-permute-start | bytes 245768 | tf_op jit(solution)/shard_map/ppermute | solution.py:14
  105.5 4.1 %collective-permute-start.21 = (f32[4,160,128]{2,1,0:T(8,128)S(1)}, f32[4,160,128]{2,1,0:T(8,128)S(1)}, u32[]{:S(2)}, u32[]{:S(2)}) collective-permute-start(f32[4,160,128]{2,1,0:T(8,128)S(1)} %bitcast_dynamic-update-slice_fusion.2), channel_id=1, source_target_pairs={{0,32},{32,0},{1,33},{33,1},{2,34},{34,2},{3,35},{35,3},{4,36},{36... | collective-permute-start | bytes 983048 | tf_op jit(solution)/shard_map/ppermute | solution.py:14
  111.0 21.2 %shard_map.45 = (f32[512,512]{1,0:T(8,128)}, f32[512,512]{1,0:T(8,128)S(1)}) custom-call(f32[10,128,128]{2,1,0:T(8,128)S(1)} %bitcast.48), custom_call_target="tpu_custom_call" | custom-call | tf_op jit(solution)/shard_map/pallas_call | solution.py:133
  132.1 9.1 %shard_map.46 = f32[8,512,512]{2,1,0:T(8,128)} custom-call(f32[8,512,512]{2,1,0:T(8,128)} %bitcast.51, f32[512,512]{1,0:T(8,128)S(1)} %get-tuple-element.40.n_ref), custom_call_target="tpu_custom_call" | custom-call | tf_op jit(solution)/shard_map/pallas_call | solution.py:514
  (72 shorter events, 23.3 us)
Async XLA Ops:
  2.9 27.3 %collective-permute-start = (f32[9,1,32,512]{3,2,1,0:T(8,128)S(1)}, f32[9,1,32,512]{3,2,1,0:T(8,128)S(1)}, u32[]{:S(2)}, u32[]{:S(2)}) collective-permute-start(f32[9,1,32,512]{3,2,1,0:T(8,128)S(1)} %pad_maximum_fusion.1.yhi), channel_id=1, source_target_pairs={{0,32},{32,64},{64,96},{1,33},{33,65},{65,97},{2,34},{34,66},{66,9... | collective-permute-start | bytes 1769480 | tf_op jit(solution)/shard_map/ppermute | solution.py:537
  9.1 21.0 %collective-permute-start.1 = (f32[9,1,32,512]{3,2,1,0:T(8,128)S(1)}, f32[9,1,32,512]{3,2,1,0:T(8,128)S(1)}, u32[]{:S(2)}, u32[]{:S(2)}) collective-permute-start(f32[9,1,32,512]{3,2,1,0:T(8,128)S(1)} %pad_maximum_fusion.ylo), channel_id=1, source_target_pairs={{32,0},{64,32},{96,64},{33,1},{65,33},{97,65},{34,2},{66,34},{98,6... | collective-permute-start | bytes 1769480 | tf_op jit(solution)/shard_map/ppermute | solution.py:537
  15.0 15.1 %collective-permute-start.2 = (f32[9,16,512]{2,1,0:T(8,128)S(1)}, f32[9,16,512]{2,1,0:T(8,128)S(1)}, u32[]{:S(2)}, u32[]{:S(2)}) collective-permute-start(f32[9,16,512]{2,1,0:T(8,128)S(1)} %pad_maximum_fusion.3.zhi), channel_id=1, source_target_pairs={{0,1},{1,2},{2,3},{3,4},{4,5},{5,6},{6,7},{7,8},{8,9},{9,10},{10,1... | collective-permute-start | bytes 884744 | tf_op jit(solution)/shard_map/ppermute | solution.py:537
  17.4 12.8 %collective-permute-start.3 = (f32[9,16,512]{2,1,0:T(8,128)S(1)}, f32[9,16,512]{2,1,0:T(8,128)S(1)}, u32[]{:S(2)}, u32[]{:S(2)}) collective-permute-start(f32[9,16,512]{2,1,0:T(8,128)S(1)} %pad_maximum_fusion.2.zlo), channel_id=1, source_target_pairs={{1,0},{2,1},{3,2},{4,3},{5,4},{6,5},{7,6},{8,7},{9,8},{10,9},{11,1... | collective-permute-start | bytes 884744 | tf_op jit(solution)/shard_map/ppermute | solution.py:537
  33.0 27.5 %collective-permute-start.4 = (f32[8,1,32,512]{3,2,1,0:T(8,128)S(1)}, f32[8,1,32,512]{3,2,1,0:T(8,128)S(1)}, u32[]{:S(2)}, u32[]{:S(2)}) collective-permute-start(f32[8,1,32,512]{3,2,1,0:T(8,128)S(1)} %get-tuple-element.31.oyhi), channel_id=1, source_target_pairs={{0,32},{32,64},{64,96},{1,33},{33,65},{65,97},{2,34},{34,66},{66,9... | collective-permute-start | bytes 1572872 | tf_op jit(solution)/shard_map/ppermute | solution.py:537
  40.8 19.7 %collective-permute-start.5 = (f32[8,1,32,512]{3,2,1,0:T(8,128)S(1)}, f32[8,1,32,512]{3,2,1,0:T(8,128)S(1)}, u32[]{:S(2)}, u32[]{:S(2)}) collective-permute-start(f32[8,1,32,512]{3,2,1,0:T(8,128)S(1)} %get-tuple-element.30.oylo), channel_id=1, source_target_pairs={{32,0},{64,32},{96,64},{33,1},{65,33},{97,65},{34,2},{66,34},{98,6... | collective-permute-start | bytes 1572872 | tf_op jit(solution)/shard_map/ppermute | solution.py:537
  42.8 15.4 %collective-permute-start.6 = (f32[8,16,512]{2,1,0:T(8,128)S(1)}, f32[8,16,512]{2,1,0:T(8,128)S(1)}, u32[]{:S(2)}, u32[]{:S(2)}) collective-permute-start(f32[8,16,512]{2,1,0:T(8,128)S(1)} %get-tuple-element.33.ozhi), channel_id=1, source_target_pairs={{0,1},{1,2},{2,3},{3,4},{4,5},{5,6},{6,7},{7,8},{8,9},{9,10},{10,1... | collective-permute-start | bytes 786440 | tf_op jit(solution)/shard_map/ppermute | solution.py:537
  45.9 13.9 %collective-permute-start.7 = (f32[8,16,512]{2,1,0:T(8,128)S(1)}, f32[8,16,512]{2,1,0:T(8,128)S(1)}, u32[]{:S(2)}, u32[]{:S(2)}) collective-permute-start(f32[8,16,512]{2,1,0:T(8,128)S(1)} %get-tuple-element.32.ozlo), channel_id=1, source_target_pairs={{1,0},{2,1},{3,2},{4,3},{5,4},{6,5},{7,6},{8,7},{9,8},{10,9},{11,1... | collective-permute-start | bytes 786440 | tf_op jit(solution)/shard_map/ppermute | solution.py:537
  47.2 13.3 %copy-start.3 = (f32[32,512]{1,0:T(8,128)S(1)}, f32[32,512]{1,0:T(8,128)}, u32[]{:S(2)}) copy-start(f32[32,512]{1,0:T(8,128)} %copy-done.2) | copy-start | bytes 196612
  47.2 13.3 %copy-start.5 = (f32[32,512]{1,0:T(8,128)S(1)}, f32[32,512]{1,0:T(8,128)}, u32[]{:S(2)}) copy-start(f32[32,512]{1,0:T(8,128)} %copy-done.4) | copy-start | bytes 196612
  69.7 1.7 %collective-permute-start.8 = (f32[4,160,128]{2,1,0:T(8,128)S(1)}, f32[4,160,128]{2,1,0:T(8,128)S(1)}, u32[]{:S(2)}, u32[]{:S(2)}) collective-permute-start(f32[4,160,128]{2,1,0:T(8,128)S(1)} %dynamic-slice_bitcast_fusion), channel_id=1, source_target_pairs={{0,32},{32,0},{1,33},{33,1},{2,34},{34,2},{3,35},{35,3},{4,36},{36... | collective-permute-start | bytes 983048 | tf_op jit(solution)/shard_map/ppermute | solution.py:14
  71.5 9.0 %collective-permute-start.10 = (f32[160,128]{1,0:T(8,128)S(1)}, f32[160,128]{1,0:T(8,128)S(1)}, u32[]{:S(2)}, u32[]{:S(2)}) collective-permute-start(f32[160,128]{1,0:T(8,128)S(1)} %get-tuple-element.54), channel_id=1, source_target_pairs={{0,64},{1,65},{64,0},{65,1},{2,66},{3,67},{66,2},{67,3},{4,68},{5,... | collective-permute-start | bytes 245768 | tf_op jit(solution)/shard_map/ppermute | solution.py:14
  78.0 4.7 %collective-permute-start.11 = (f32[160,128]{1,0:T(8,128)S(1)}, f32[160,128]{1,0:T(8,128)S(1)}, u32[]{:S(2)}, u32[]{:S(2)}) collective-permute-start(f32[160,128]{1,0:T(8,128)S(1)} %get-tuple-element.53), channel_id=1, source_target_pairs={{0,65},{1,0},{64,1},{65,64},{2,67},{3,2},{66,3},{67,66},{4,69},{5,... | collective-permute-start | bytes 245768 | tf_op jit(solution)/shard_map/ppermute | solution.py:14
  78.4 4.5 %collective-permute-start.9 = (f32[160,128]{1,0:T(8,128)S(1)}, f32[160,128]{1,0:T(8,128)S(1)}, u32[]{:S(2)}, u32[]{:S(2)}) collective-permute-start(f32[160,128]{1,0:T(8,128)S(1)} %get-tuple-element.52), channel_id=1, source_target_pairs={{0,1},{1,64},{64,65},{65,0},{2,3},{3,66},{66,67},{67,2},{4,5},{5,6... | collective-permute-start | bytes 245768 | tf_op jit(solution)/shard_map/ppermute | solution.py:14
  82.9 5.0 %collective-permute-start.12 = (f32[160,128]{1,0:T(8,128)S(1)}, f32[160,128]{1,0:T(8,128)S(1)}, u32[]{:S(2)}, u32[]{:S(2)}) collective-permute-start(f32[160,128]{1,0:T(8,128)S(1)} %fusion.1), channel_id=1, source_target_pairs={{0,2},{2,4},{4,6},{6,0},{1,3},{3,5},{5,7},{7,1},{8,10},{10,12},{12... | collective-permute-start | bytes 245768 | tf_op jit(solution)/shard_map/ppermute | solution.py:14
  84.3 5.2 %collective-permute-start.13 = (f32[160,128]{1,0:T(8,128)S(1)}, f32[160,128]{1,0:T(8,128)S(1)}, u32[]{:S(2)}, u32[]{:S(2)}) collective-permute-start(f32[160,128]{1,0:T(8,128)S(1)} %fusion.1), channel_id=1, source_target_pairs={{0,4},{2,6},{4,0},{6,2},{1,5},{3,7},{5,1},{7,3},{8,12},{10,14},{12... | collective-permute-start | bytes 245768 | tf_op jit(solution)/shard_map/ppermute | solution.py:14
  85.9 4.2 %collective-permute-start.14 = (f32[160,128]{1,0:T(8,128)S(1)}, f32[160,128]{1,0:T(8,128)S(1)}, u32[]{:S(2)}, u32[]{:S(2)}) collective-permute-start(f32[160,128]{1,0:T(8,128)S(1)} %fusion.1), channel_id=1, source_target_pairs={{0,6},{2,0},{4,2},{6,4},{1,7},{3,1},{5,3},{7,5},{8,14},{10,8},{12,... | collective-permute-start | bytes 245768 | tf_op jit(solution)/shard_map/ppermute | solution.py:14
  90.2 4.6 %collective-permute-start.15 = (f32[160,128]{1,0:T(8,128)S(1)}, f32[160,128]{1,0:T(8,128)S(1)}, u32[]{:S(2)}, u32[]{:S(2)}) collective-permute-start(f32[160,128]{1,0:T(8,128)S(1)} %add_add_fusion.1), channel_id=1, source_target_pairs={{0,8},{8,16},{16,24},{24,0},{1,9},{9,17},{17,25},{25,1},{2,10},{10... | collective-permute-start | bytes 245768 | tf_op jit(solution)/shard_map/ppermute | solution.py:14
  91.1 5.2 %collective-permute-start.16 = (f32[160,128]{1,0:T(8,128)S(1)}, f32[160,128]{1,0:T(8,128)S(1)}, u32[]{:S(2)}, u32[]{:S(2)}) collective-permute-start(f32[160,128]{1,0:T(8,128)S(1)} %add_add_fusion.1), channel_id=1, source_target_pairs={{0,16},{8,24},{16,0},{24,8},{1,17},{9,25},{17,1},{25,9},{2,18},{10... | collective-permute-start | bytes 245768 | tf_op jit(solution)/shard_map/ppermute | solution.py:14
  93.6 3.6 %collective-permute-start.17 = (f32[160,128]{1,0:T(8,128)S(1)}, f32[160,128]{1,0:T(8,128)S(1)}, u32[]{:S(2)}, u32[]{:S(2)}) collective-permute-start(f32[160,128]{1,0:T(8,128)S(1)} %add_add_fusion.1), channel_id=1, source_target_pairs={{0,24},{8,0},{16,8},{24,16},{1,25},{9,1},{17,9},{25,17},{2,26},{10... | collective-permute-start | bytes 245768 | tf_op jit(solution)/shard_map/ppermute | solution.py:14
  97.2 6.8 %collective-permute-start.18 = (f32[160,128]{1,0:T(8,128)S(1)}, f32[160,128]{1,0:T(8,128)S(1)}, u32[]{:S(2)}, u32[]{:S(2)}) collective-permute-start(f32[160,128]{1,0:T(8,128)S(1)} %get-tuple-element.43), channel_id=1, source_target_pairs={{0,1},{1,64},{64,65},{65,0},{2,3},{3,66},{66,67},{67,2},{4,5},{5,6... | collective-permute-start | bytes 245768 | tf_op jit(solution)/shard_map/ppermute | solution.py:14
  97.9 6.7 %collective-permute-start.19 = (f32[160,128]{1,0:T(8,128)S(1)}, f32[160,128]{1,0:T(8,128)S(1)}, u32[]{:S(2)}, u32[]{:S(2)}) collective-permute-start(f32[160,128]{1,0:T(8,128)S(1)} %get-tuple-element.43), channel_id=1, source_target_pairs={{0,64},{1,65},{64,0},{65,1},{2,66},{3,67},{66,2},{67,3},{4,68},{5,... | collective-permute-start | bytes 245768 | tf_op jit(solution)/shard_map/ppermute | solution.py:14
  102.1 3.4 %collective-permute-start.20 = (f32[160,128]{1,0:T(8,128)S(1)}, f32[160,128]{1,0:T(8,128)S(1)}, u32[]{:S(2)}, u32[]{:S(2)}) collective-permute-start(f32[160,128]{1,0:T(8,128)S(1)} %get-tuple-element.43), channel_id=1, source_target_pairs={{0,65},{1,0},{64,1},{65,64},{2,67},{3,2},{66,3},{67,66},{4,69},{5,... | collective-permute-start | bytes 245768 | tf_op jit(solution)/shard_map/ppermute | solution.py:14
  105.5 5.4 %collective-permute-start.21 = (f32[4,160,128]{2,1,0:T(8,128)S(1)}, f32[4,160,128]{2,1,0:T(8,128)S(1)}, u32[]{:S(2)}, u32[]{:S(2)}) collective-permute-start(f32[4,160,128]{2,1,0:T(8,128)S(1)} %bitcast_dynamic-update-slice_fusion.2), channel_id=1, source_target_pairs={{0,32},{32,0},{1,33},{33,1},{2,34},{34,2},{3,35},{35,3},{4,36},{36... | collective-permute-start | bytes 983048 | tf_op jit(solution)/shard_map/ppermute | solution.py:14
  (8 other events, 30.7 us)

commit v3 on v2

--- a/solution.py
+++ b/solution.py
@@ -127,19 +127,6 @@
                 n_ref[a:a+BLK,a:n]=n_ref[a:a+BLK,a:n]-upw[a-hi:a-hi+BLK,a-hi:]
 
 
-def factor_and_inverse(blocks, n):
-    square = jax.ShapeDtypeStruct((n, n), jnp.float32)
-    whole = pl.BlockSpec(memory_space=pltpu.VMEM)
-    return pl.pallas_call(
-        factor_kernel,
-        out_shape=(square, square),
-        in_specs=[whole],
-        out_specs=(whole, whole),
-        scratch_shapes=[pltpu.VMEM((BLK, 2 * BLK), jnp.float32)],
-        compiler_params=pltpu.CompilerParams(vmem_limit_bytes=24 * 2**20),
-    )(blocks)
-
-
 def ahead(a, axis):
     return pltpu.roll(a, a.shape[axis] - 1, axis)
 
@@ -471,7 +458,7 @@
     )(t, *faces, *halos, *links)
 
 
-def basis_kernel(r_far, n_ref, o_far, rbuf, obuf, high, low, r_sem, o_sem):
+def finish_kernel(g_ref, r_far, fac_ref, o_far, n_ref, panel, rbuf, obuf, high, low, r_sem, o_sem):
     count, chunk, width = rbuf.shape
     step = 256
 
@@ -481,14 +468,16 @@
     def store(i):
         return pltpu.make_async_copy(obuf.at[i], o_far.at[i], o_sem.at[i])
 
-    def work(i):
-        @pl.when(i == 0)
-        def _():
-            n = n_ref[...]
-            h = n.astype(jnp.bfloat16)
-            high[...] = h
-            low[...] = (n - h.astype(jnp.float32)).astype(jnp.bfloat16)
-
+    for i in range(count):
+        fetch(i).start()
+    factor_kernel(g_ref, fac_ref, n_ref, panel)
+    n = n_ref[...]
+    h = n.astype(jnp.bfloat16)
+    high[...] = h
+    low[...] = (n - h.astype(jnp.float32)).astype(jnp.bfloat16)
+
+    def project(i, carry):
+        fetch(i).wait()
         r = rbuf[i]
         a = r.astype(jnp.bfloat16)
         b = (r - a.astype(jnp.float32)).astype(jnp.bfloat16)
@@ -501,24 +490,28 @@
                 )
 
             obuf[i, :, lo:hi] = times(a, high) + (times(a, low) + times(b, high))
-
-    stream(count, fetch, work, store)
+        store(i).start()
+        return carry
+
+    lax.fori_loop(0, count, project, 0)
     drain(count, store)
 
 
-def basis_of(rows, inverse_t, chunk=512):
+def factor_and_basis(blocks, rows, chunk=512):
     m, nx = rows.shape
     cut = (m // chunk, chunk, nx)
     big = pltpu.VMEM(cut, jnp.float32)
     sem = pltpu.SemaphoreType.DMA((m // chunk,))
     return pl.pallas_call(
-        basis_kernel,
-        in_specs=[FAR, NEAR],
-        out_specs=FAR,
-        out_shape=pltpu.HBM(cut, jnp.float32),
-        scratch_shapes=[big, big] + [pltpu.VMEM((nx, nx), jnp.bfloat16)] * 2 + [sem, sem],
+        finish_kernel,
+        in_specs=[NEAR, FAR],
+        out_specs=(NEAR, FAR),
+        out_shape=(jax.ShapeDtypeStruct((nx, nx), jnp.float32), pltpu.HBM(cut, jnp.float32)),
+        scratch_shapes=[pltpu.VMEM((nx, nx), jnp.float32), pltpu.VMEM((BLK, 2 * BLK), jnp.float32), big, big]
+        + [pltpu.VMEM((nx, nx), jnp.bfloat16)] * 2
+        + [sem, sem],
         compiler_params=limit(32),
-    )(far(rows.reshape(cut)), inverse_t)
+    )(blocks, far(rows.reshape(cut)))
 
 
 BY = ("yh", "c")
@@ -559,8 +552,7 @@
     relaxed, blocks = edge_relax(twice, faces, halo, links)
     total_rows = nfield * ny * axis_count(BY) * nz * axis_count(BZ)
     blocks = sum_over_devices(blocks) / jnp.float32(total_rows)
-    factor, inverse_t = factor_and_inverse(blocks, width)
-    basis = basis_of(relaxed.reshape(-1, width), inverse_t)
+    factor, basis = factor_and_basis(blocks, relaxed.reshape(-1, width))
     return (basis.reshape(relaxed.shape), factor)
 
 

time: 142 us -> 141 us (level)
    pallas_call x2 -> x1, Pallas kernels: 30.2 us -> 29.4 us  [factor_and_basis(): pl.pallas_call(finish_kernel, in_specs=[NEAR, FAR], out_specs=(NEAR, FAR)...]
where the time goes in v3:
time: 141 us
  Pallas kernels  59.1 us (42%)
  starting transfers between devices  54.3 us (39%)
  waiting for transfers between devices  15.3 us (11%)
  local copies, waits for them, and re-layouts  10.4 us (7%)
    pallas_call x1, Pallas kernels, factor_and_basis(): pl.pallas_call(finish_kernel, in_specs=[NEAR, FAR], out_specs=(NEAR, FAR)...  29.4 us
    ppermute x14, starting transfers between devices, shifted(): lax.ppermute(piece, axes, [(i, (i + distance) % count) for i in range(cou...  28.5 us
    ppermute x8, starting transfers between devices, from_next(): lax.ppermute(piece, axes, [(i + step, i) for i in range(n) if 0 <= i + st...  25.9 us
    ppermute x14, waiting for transfers between devices, shifted(): lax.ppermute(piece, axes, [(i, (i + distance) % count) for i in range(cou...  12.4 us
    pallas_call x1, Pallas kernels, own_relax(): pl.pallas_call(own_kernel, in_specs=[FAR, FAR], out_specs=(FAR,) * 4 + (N...  11.4 us
    pallas_call x1, Pallas kernels, again_relax(): pl.pallas_call(again_kernel, in_specs=[FAR] * 4 + [NEAR] * 4, out_specs=N...  9.71 us
    pallas_call x1, Pallas kernels, edge_relax(): pl.pallas_call(edge_kernel, in_specs=[NEAR] * 13, out_specs=(FAR, NEAR),...  8.14 us
    unnamed x24, local copies, waits for them, and re-layouts  4.14 us
  transfers between devices with their start and end apart: 22, of which 13 were waited for; matrix products, arithmetic and copies ran while one was open for 3% of the time, Pallas kernels for 15%

profile of v3, /device:TPU:1, one launch (start us, length us, event | category | flops | bytes accessed | tf_op | source)
XLA Modules:
  0.0 140.6 jit_solution(3811553337244396498)
XLA Ops:
  2.9 6.2 %collective-permute-start = (f32[9,1,32,512]{3,2,1,0:T(8,128)S(1)}, f32[9,1,32,512]{3,2,1,0:T(8,128)S(1)}, u32[]{:S(2)}, u32[]{:S(2)}) collective-permute-start(f32[9,1,32,512]{3,2,1,0:T(8,128)S(1)} %pad_maximum_fusion.1.yhi), channel_id=1, source_target_pairs={{0,32},{32,64},{64,96},{1,33},{33,65},{65,97},{2,34},{34,66},{66,9... | collective-permute-start | bytes 1769480 | tf_op jit(solution)/shard_map/ppermute | solution.py:530
  9.1 1.9 %collective-permute-start.1 = (f32[9,1,32,512]{3,2,1,0:T(8,128)S(1)}, f32[9,1,32,512]{3,2,1,0:T(8,128)S(1)}, u32[]{:S(2)}, u32[]{:S(2)}) collective-permute-start(f32[9,1,32,512]{3,2,1,0:T(8,128)S(1)} %pad_maximum_fusion.ylo), channel_id=1, source_target_pairs={{32,0},{64,32},{96,64},{33,1},{65,33},{97,65},{34,2},{66,34},{98,6... | collective-permute-start | bytes 1769480 | tf_op jit(solution)/shard_map/ppermute | solution.py:530
  11.1 2.8 %fusion.2 = (f32[8,16,1,512]{3,2,1,0:T(1,128)S(1)}, f32[8,16,1,512]{3,2,1,0:T(1,128)S(1)}) fusion(f32[8,16,32,512]{3,2,1,0:T(8,128)} %f_far.1), kind=kLoop, calls=%fused_computation.27 | loop fusion | bytes 1048576 | tf_op jit(solution)/shard_map/slice | solution.py:537
  15.0 2.3 %collective-permute-start.2 = (f32[9,16,512]{2,1,0:T(8,128)S(1)}, f32[9,16,512]{2,1,0:T(8,128)S(1)}, u32[]{:S(2)}, u32[]{:S(2)}) collective-permute-start(f32[9,16,512]{2,1,0:T(8,128)S(1)} %pad_maximum_fusion.3.zhi), channel_id=1, source_target_pairs={{0,1},{1,2},{2,3},{3,4},{4,5},{5,6},{6,7},{7,8},{8,9},{9,10},{10,1... | collective-permute-start | bytes 884744 | tf_op jit(solution)/shard_map/ppermute | solution.py:530
  18.7 11.4 %shard_map.41 = (f32[8,16,32,512]{3,2,1,0:T(8,128)}, f32[16,32,512]{2,1,0:T(8,128)}, f32[16,32,512]{2,1,0:T(8,128)}, f32[16,32,512]{2,1,0:T(8,128)}, f32[8,1,32,...) custom-call(f32[8,16,32,512]{3,2,1,0:T(8,128)} %f_far.1, ...), custom_call_target="tpu_custom_call" | custom-call | tf_op jit(solution)/shard_map/pallas_call | solution.py:283
  33.0 7.8 %collective-permute-start.4 = (f32[8,1,32,512]{3,2,1,0:T(8,128)S(1)}, f32[8,1,32,512]{3,2,1,0:T(8,128)S(1)}, u32[]{:S(2)}, u32[]{:S(2)}) collective-permute-start(f32[8,1,32,512]{3,2,1,0:T(8,128)S(1)} %get-tuple-element.31.oyhi), channel_id=1, source_target_pairs={{0,32},{32,64},{64,96},{1,33},{33,65},{65,97},{2,34},{34,66},{66,9... | collective-permute-start | bytes 1572872 | tf_op jit(solution)/shard_map/ppermute | solution.py:530
  40.8 1.9 %collective-permute-start.5 = (f32[8,1,32,512]{3,2,1,0:T(8,128)S(1)}, f32[8,1,32,512]{3,2,1,0:T(8,128)S(1)}, u32[]{:S(2)}, u32[]{:S(2)}) collective-permute-start(f32[8,1,32,512]{3,2,1,0:T(8,128)S(1)} %get-tuple-element.30.oylo), channel_id=1, source_target_pairs={{32,0},{64,32},{96,64},{33,1},{65,33},{97,65},{34,2},{66,34},{98,6... | collective-permute-start | bytes 1572872 | tf_op jit(solution)/shard_map/ppermute | solution.py:530
  42.8 3.1 %collective-permute-start.6 = (f32[8,16,512]{2,1,0:T(8,128)S(1)}, f32[8,16,512]{2,1,0:T(8,128)S(1)}, u32[]{:S(2)}, u32[]{:S(2)}) collective-permute-start(f32[8,16,512]{2,1,0:T(8,128)S(1)} %get-tuple-element.33.ozhi), channel_id=1, source_target_pairs={{0,1},{1,2},{2,3},{3,4},{4,5},{5,6},{6,7},{7,8},{8,9},{9,10},{10,1... | collective-permute-start | bytes 786440 | tf_op jit(solution)/shard_map/ppermute | solution.py:530
  47.3 9.7 %shard_map.43.t_ref = f32[8,16,32,512]{3,2,1,0:T(8,128)S(1)} custom-call(f32[8,16,32,512]{3,2,1,0:T(8,128)} %get-tuple-element.22.p_far, f32[16,32,512]{2,1,0:T(8,128)} %get-tuple-element.23.wx_far, f32[16,32,512]{2,1,0:T(8,128)} %get-tuple-element.24.wy_far, f32[16,32,512]{2,1,0:T(8,128)} %get-tuple-element.25.wz_far, ...), custom_call_target="tpu_custom_call" | custom-call | tf_op jit(solution)/shard_map/pallas_call | solution.py:377
  58.2 1.7 %collective-permute-done.7.zr = f32[8,16,512]{2,1,0:T(8,128)S(1)} collective-permute-done((f32[8,16,512]{2,1,0:T(8,128)S(1)}, f32[8,16,512]{2,1,0:T(8,128)S(1)}, u32[]{:S(2)}, u32[]{:S(2)}) %collective-permute-start.7) | collective-permute-done | bytes 262176 | tf_op jit(solution)/shard_map/ppermute | solution.py:530
  61.5 8.1 %shard_map.44 = (f32[8,16,32,512]{3,2,1,0:T(8,128)}, f32[10,128,128]{2,1,0:T(8,128)S(1)}) custom-call(f32[8,16,32,512]{3,2,1,0:T(8,128)S(1)} %shard_map.43.t_ref, f32[8,1,32,512]{3,2,1,0:T(8,128)S(1)} %get-tuple-element.30.oylo, f32[8,1,32,512]{3,2,1,0:T(8,128)S(1)} %get-tuple-element.31.oyhi, f32[8,16,512]{2,1,0:T(8,128)S(1)} %get-tuple-element.32.ozlo, ...), custom_call_target="tpu_custom_call" | custom-call | tf_op jit(solution)/shard_map/pallas_call | solution.py:446
  69.8 1.6 %collective-permute-done.8 = f32[4,160,128]{2,1,0:T(8,128)S(1)} collective-permute-done((f32[4,160,128]{2,1,0:T(8,128)S(1)}, f32[4,160,128]{2,1,0:T(8,128)S(1)}, u32[]{:S(2)}, u32[]{:S(2)}) %collective-permute-start.8) | collective-permute-done | bytes 327712 | tf_op jit(solution)/shard_map/ppermute | solution.py:14
  71.5 6.5 %collective-permute-start.10 = (f32[160,128]{1,0:T(8,128)S(1)}, f32[160,128]{1,0:T(8,128)S(1)}, u32[]{:S(2)}, u32[]{:S(2)}) collective-permute-start(f32[160,128]{1,0:T(8,128)S(1)} %get-tuple-element.54), channel_id=1, source_target_pairs={{0,64},{1,65},{64,0},{65,1},{2,66},{3,67},{66,2},{67,3},{4,68},{5,... | collective-permute-start | bytes 245768 | tf_op jit(solution)/shard_map/ppermute | solution.py:14
  80.5 2.2 %collective-permute-done.11 = f32[160,128]{1,0:T(8,128)S(1)} collective-permute-done((f32[160,128]{1,0:T(8,128)S(1)}, f32[160,128]{1,0:T(8,128)S(1)}, u32[]{:S(2)}, u32[]{:S(2)}) %collective-permute-start.11) | collective-permute-done | bytes 81952 | tf_op jit(solution)/shard_map/ppermute | solution.py:14
  82.9 1.4 %collective-permute-start.12 = (f32[160,128]{1,0:T(8,128)S(1)}, f32[160,128]{1,0:T(8,128)S(1)}, u32[]{:S(2)}, u32[]{:S(2)}) collective-permute-start(f32[160,128]{1,0:T(8,128)S(1)} %fusion.1), channel_id=1, source_target_pairs={{0,2},{2,4},{4,6},{6,0},{1,3},{3,5},{5,7},{7,1},{8,10},{10,12},{12... | collective-permute-start | bytes 245768 | tf_op jit(solution)/shard_map/ppermute | solution.py:14
  84.3 1.6 %collective-permute-start.13 = (f32[160,128]{1,0:T(8,128)S(1)}, f32[160,128]{1,0:T(8,128)S(1)}, u32[]{:S(2)}, u32[]{:S(2)}) collective-permute-start(f32[160,128]{1,0:T(8,128)S(1)} %fusion.1), channel_id=1, source_target_pairs={{0,4},{2,6},{4,0},{6,2},{1,5},{3,7},{5,1},{7,3},{8,12},{10,14},{12... | collective-permute-start | bytes 245768 | tf_op jit(solution)/shard_map/ppermute | solution.py:14
  85.9 2.0 %collective-permute-start.14 = (f32[160,128]{1,0:T(8,128)S(1)}, f32[160,128]{1,0:T(8,128)S(1)}, u32[]{:S(2)}, u32[]{:S(2)}) collective-permute-start(f32[160,128]{1,0:T(8,128)S(1)} %fusion.1), channel_id=1, source_target_pairs={{0,6},{2,0},{4,2},{6,4},{1,7},{3,1},{5,3},{7,5},{8,14},{10,8},{12,... | collective-permute-start | bytes 245768 | tf_op jit(solution)/shard_map/ppermute | solution.py:14
  87.9 1.6 %collective-permute-done.13 = f32[160,128]{1,0:T(8,128)S(1)} collective-permute-done((f32[160,128]{1,0:T(8,128)S(1)}, f32[160,128]{1,0:T(8,128)S(1)}, u32[]{:S(2)}, u32[]{:S(2)}) %collective-permute-start.13) | collective-permute-done | bytes 81952 | tf_op jit(solution)/shard_map/ppermute | solution.py:14
  91.1 2.5 %collective-permute-start.16 = (f32[160,128]{1,0:T(8,128)S(1)}, f32[160,128]{1,0:T(8,128)S(1)}, u32[]{:S(2)}, u32[]{:S(2)}) collective-permute-start(f32[160,128]{1,0:T(8,128)S(1)} %add_add_fusion.1), channel_id=1, source_target_pairs={{0,16},{8,24},{16,0},{24,8},{1,17},{9,25},{17,1},{25,9},{2,18},{10... | collective-permute-start | bytes 245768 | tf_op jit(solution)/shard_map/ppermute | solution.py:14
  94.8 1.5 %collective-permute-done.16 = f32[160,128]{1,0:T(8,128)S(1)} collective-permute-done((f32[160,128]{1,0:T(8,128)S(1)}, f32[160,128]{1,0:T(8,128)S(1)}, u32[]{:S(2)}, u32[]{:S(2)}) %collective-permute-start.16) | collective-permute-done | bytes 81952 | tf_op jit(solution)/shard_map/ppermute | solution.py:14
  97.9 4.2 %collective-permute-start.19 = (f32[160,128]{1,0:T(8,128)S(1)}, f32[160,128]{1,0:T(8,128)S(1)}, u32[]{:S(2)}, u32[]{:S(2)}) collective-permute-start(f32[160,128]{1,0:T(8,128)S(1)} %get-tuple-element.43), channel_id=1, source_target_pairs={{0,64},{1,65},{64,0},{65,1},{2,66},{3,67},{66,2},{67,3},{4,68},{5,... | collective-permute-start | bytes 245768 | tf_op jit(solution)/shard_map/ppermute | solution.py:14
  102.1 1.9 %collective-permute-start.20 = (f32[160,128]{1,0:T(8,128)S(1)}, f32[160,128]{1,0:T(8,128)S(1)}, u32[]{:S(2)}, u32[]{:S(2)}) collective-permute-start(f32[160,128]{1,0:T(8,128)S(1)} %get-tuple-element.43), channel_id=1, source_target_pairs={{0,65},{1,0},{64,1},{65,64},{2,67},{3,2},{66,3},{67,66},{4,69},{5,... | collective-permute-start | bytes 245768 | tf_op jit(solution)/shard_map/ppermute | solution.py:14
  105.5 4.1 %collective-permute-start.21 = (f32[4,160,128]{2,1,0:T(8,128)S(1)}, f32[4,160,128]{2,1,0:T(8,128)S(1)}, u32[]{:S(2)}, u32[]{:S(2)}) collective-permute-start(f32[4,160,128]{2,1,0:T(8,128)S(1)} %bitcast_dynamic-update-slice_fusion.2), channel_id=1, source_target_pairs={{0,32},{32,0},{1,33},{33,1},{2,34},{34,2},{3,35},{35,3},{4,36},{36... | collective-permute-start | bytes 983048 | tf_op jit(solution)/shard_map/ppermute | solution.py:14
  111.0 29.4 %shard_map.45 = (f32[512,512]{1,0:T(8,128)}, f32[8,512,512]{2,1,0:T(8,128)}) custom-call(f32[10,128,128]{2,1,0:T(8,128)S(1)} %bitcast.48, f32[8,512,512]{2,1,0:T(8,128)} %bitcast.51), custom_call_target="tpu_custom_call" | custom-call | tf_op jit(solution)/shard_map/pallas_call | solution.py:505
  (71 shorter events, 21.9 us)
Async XLA Ops:
  2.9 27.3 %collective-permute-start = (f32[9,1,32,512]{3,2,1,0:T(8,128)S(1)}, f32[9,1,32,512]{3,2,1,0:T(8,128)S(1)}, u32[]{:S(2)}, u32[]{:S(2)}) collective-permute-start(f32[9,1,32,512]{3,2,1,0:T(8,128)S(1)} %pad_maximum_fusion.1.yhi), channel_id=1, source_target_pairs={{0,32},{32,64},{64,96},{1,33},{33,65},{65,97},{2,34},{34,66},{66,9... | collective-permute-start | bytes 1769480 | tf_op jit(solution)/shard_map/ppermute | solution.py:530
  9.1 21.0 %collective-permute-start.1 = (f32[9,1,32,512]{3,2,1,0:T(8,128)S(1)}, f32[9,1,32,512]{3,2,1,0:T(8,128)S(1)}, u32[]{:S(2)}, u32[]{:S(2)}) collective-permute-start(f32[9,1,32,512]{3,2,1,0:T(8,128)S(1)} %pad_maximum_fusion.ylo), channel_id=1, source_target_pairs={{32,0},{64,32},{96,64},{33,1},{65,33},{97,65},{34,2},{66,34},{98,6... | collective-permute-start | bytes 1769480 | tf_op jit(solution)/shard_map/ppermute | solution.py:530
  15.0 15.1 %collective-permute-start.2 = (f32[9,16,512]{2,1,0:T(8,128)S(1)}, f32[9,16,512]{2,1,0:T(8,128)S(1)}, u32[]{:S(2)}, u32[]{:S(2)}) collective-permute-start(f32[9,16,512]{2,1,0:T(8,128)S(1)} %pad_maximum_fusion.3.zhi), channel_id=1, source_target_pairs={{0,1},{1,2},{2,3},{3,4},{4,5},{5,6},{6,7},{7,8},{8,9},{9,10},{10,1... | collective-permute-start | bytes 884744 | tf_op jit(solution)/shard_map/ppermute | solution.py:530
  17.4 12.8 %collective-permute-start.3 = (f32[9,16,512]{2,1,0:T(8,128)S(1)}, f32[9,16,512]{2,1,0:T(8,128)S(1)}, u32[]{:S(2)}, u32[]{:S(2)}) collective-permute-start(f32[9,16,512]{2,1,0:T(8,128)S(1)} %pad_maximum_fusion.2.zlo), channel_id=1, source_target_pairs={{1,0},{2,1},{3,2},{4,3},{5,4},{6,5},{7,6},{8,7},{9,8},{10,9},{11,1... | collective-permute-start | bytes 884744 | tf_op jit(solution)/shard_map/ppermute | solution.py:530
  33.0 27.5 %collective-permute-start.4 = (f32[8,1,32,512]{3,2,1,0:T(8,128)S(1)}, f32[8,1,32,512]{3,2,1,0:T(8,128)S(1)}, u32[]{:S(2)}, u32[]{:S(2)}) collective-permute-start(f32[8,1,32,512]{3,2,1,0:T(8,128)S(1)} %get-tuple-element.31.oyhi), channel_id=1, source_target_pairs={{0,32},{32,64},{64,96},{1,33},{33,65},{65,97},{2,34},{34,66},{66,9... | collective-permute-start | bytes 1572872 | tf_op jit(solution)/shard_map/ppermute | solution.py:530
  40.8 19.7 %collective-permute-start.5 = (f32[8,1,32,512]{3,2,1,0:T(8,128)S(1)}, f32[8,1,32,512]{3,2,1,0:T(8,128)S(1)}, u32[]{:S(2)}, u32[]{:S(2)}) collective-permute-start(f32[8,1,32,512]{3,2,1,0:T(8,128)S(1)} %get-tuple-element.30.oylo), channel_id=1, source_target_pairs={{32,0},{64,32},{96,64},{33,1},{65,33},{97,65},{34,2},{66,34},{98,6... | collective-permute-start | bytes 1572872 | tf_op jit(solution)/shard_map/ppermute | solution.py:530
  42.8 15.4 %collective-permute-start.6 = (f32[8,16,512]{2,1,0:T(8,128)S(1)}, f32[8,16,512]{2,1,0:T(8,128)S(1)}, u32[]{:S(2)}, u32[]{:S(2)}) collective-permute-start(f32[8,16,512]{2,1,0:T(8,128)S(1)} %get-tuple-element.33.ozhi), channel_id=1, source_target_pairs={{0,1},{1,2},{2,3},{3,4},{4,5},{5,6},{6,7},{7,8},{8,9},{9,10},{10,1... | collective-permute-start | bytes 786440 | tf_op jit(solution)/shard_map/ppermute | solution.py:530
  45.9 13.9 %collective-permute-start.7 = (f32[8,16,512]{2,1,0:T(8,128)S(1)}, f32[8,16,512]{2,1,0:T(8,128)S(1)}, u32[]{:S(2)}, u32[]{:S(2)}) collective-permute-start(f32[8,16,512]{2,1,0:T(8,128)S(1)} %get-tuple-element.32.ozlo), channel_id=1, source_target_pairs={{1,0},{2,1},{3,2},{4,3},{5,4},{6,5},{7,6},{8,7},{9,8},{10,9},{11,1... | collective-permute-start | bytes 786440 | tf_op jit(solution)/shard_map/ppermute | solution.py:530
  47.2 13.3 %copy-start.3 = (f32[32,512]{1,0:T(8,128)S(1)}, f32[32,512]{1,0:T(8,128)}, u32[]{:S(2)}) copy-start(f32[32,512]{1,0:T(8,128)} %copy-done.2) | copy-start | bytes 196612
  47.2 13.3 %copy-start.5 = (f32[32,512]{1,0:T(8,128)S(1)}, f32[32,512]{1,0:T(8,128)}, u32[]{:S(2)}) copy-start(f32[32,512]{1,0:T(8,128)} %copy-done.4) | copy-start | bytes 196612
  69.7 1.7 %collective-permute-start.8 = (f32[4,160,128]{2,1,0:T(8,128)S(1)}, f32[4,160,128]{2,1,0:T(8,128)S(1)}, u32[]{:S(2)}, u32[]{:S(2)}) collective-permute-start(f32[4,160,128]{2,1,0:T(8,128)S(1)} %dynamic-slice_bitcast_fusion), channel_id=1, source_target_pairs={{0,32},{32,0},{1,33},{33,1},{2,34},{34,2},{3,35},{35,3},{4,36},{36... | collective-permute-start | bytes 983048 | tf_op jit(solution)/shard_map/ppermute | solution.py:14
  71.5 9.0 %collective-permute-start.10 = (f32[160,128]{1,0:T(8,128)S(1)}, f32[160,128]{1,0:T(8,128)S(1)}, u32[]{:S(2)}, u32[]{:S(2)}) collective-permute-start(f32[160,128]{1,0:T(8,128)S(1)} %get-tuple-element.54), channel_id=1, source_target_pairs={{0,64},{1,65},{64,0},{65,1},{2,66},{3,67},{66,2},{67,3},{4,68},{5,... | collective-permute-start | bytes 245768 | tf_op jit(solution)/shard_map/ppermute | solution.py:14
  78.0 4.7 %collective-permute-start.11 = (f32[160,128]{1,0:T(8,128)S(1)}, f32[160,128]{1,0:T(8,128)S(1)}, u32[]{:S(2)}, u32[]{:S(2)}) collective-permute-start(f32[160,128]{1,0:T(8,128)S(1)} %get-tuple-element.53), channel_id=1, source_target_pairs={{0,65},{1,0},{64,1},{65,64},{2,67},{3,2},{66,3},{67,66},{4,69},{5,... | collective-permute-start | bytes 245768 | tf_op jit(solution)/shard_map/ppermute | solution.py:14
  78.4 4.5 %collective-permute-start.9 = (f32[160,128]{1,0:T(8,128)S(1)}, f32[160,128]{1,0:T(8,128)S(1)}, u32[]{:S(2)}, u32[]{:S(2)}) collective-permute-start(f32[160,128]{1,0:T(8,128)S(1)} %get-tuple-element.52), channel_id=1, source_target_pairs={{0,1},{1,64},{64,65},{65,0},{2,3},{3,66},{66,67},{67,2},{4,5},{5,6... | collective-permute-start | bytes 245768 | tf_op jit(solution)/shard_map/ppermute | solution.py:14
  82.9 5.0 %collective-permute-start.12 = (f32[160,128]{1,0:T(8,128)S(1)}, f32[160,128]{1,0:T(8,128)S(1)}, u32[]{:S(2)}, u32[]{:S(2)}) collective-permute-start(f32[160,128]{1,0:T(8,128)S(1)} %fusion.1), channel_id=1, source_target_pairs={{0,2},{2,4},{4,6},{6,0},{1,3},{3,5},{5,7},{7,1},{8,10},{10,12},{12... | collective-permute-start | bytes 245768 | tf_op jit(solution)/shard_map/ppermute | solution.py:14
  84.3 5.2 %collective-permute-start.13 = (f32[160,128]{1,0:T(8,128)S(1)}, f32[160,128]{1,0:T(8,128)S(1)}, u32[]{:S(2)}, u32[]{:S(2)}) collective-permute-start(f32[160,128]{1,0:T(8,128)S(1)} %fusion.1), channel_id=1, source_target_pairs={{0,4},{2,6},{4,0},{6,2},{1,5},{3,7},{5,1},{7,3},{8,12},{10,14},{12... | collective-permute-start | bytes 245768 | tf_op jit(solution)/shard_map/ppermute | solution.py:14
  85.9 4.2 %collective-permute-start.14 = (f32[160,128]{1,0:T(8,128)S(1)}, f32[160,128]{1,0:T(8,128)S(1)}, u32[]{:S(2)}, u32[]{:S(2)}) collective-permute-start(f32[160,128]{1,0:T(8,128)S(1)} %fusion.1), channel_id=1, source_target_pairs={{0,6},{2,0},{4,2},{6,4},{1,7},{3,1},{5,3},{7,5},{8,14},{10,8},{12,... | collective-permute-start | bytes 245768 | tf_op jit(solution)/shard_map/ppermute | solution.py:14
  90.2 4.6 %collective-permute-start.15 = (f32[160,128]{1,0:T(8,128)S(1)}, f32[160,128]{1,0:T(8,128)S(1)}, u32[]{:S(2)}, u32[]{:S(2)}) collective-permute-start(f32[160,128]{1,0:T(8,128)S(1)} %add_add_fusion.1), channel_id=1, source_target_pairs={{0,8},{8,16},{16,24},{24,0},{1,9},{9,17},{17,25},{25,1},{2,10},{10... | collective-permute-start | bytes 245768 | tf_op jit(solution)/shard_map/ppermute | solution.py:14
  91.1 5.2 %collective-permute-start.16 = (f32[160,128]{1,0:T(8,128)S(1)}, f32[160,128]{1,0:T(8,128)S(1)}, u32[]{:S(2)}, u32[]{:S(2)}) collective-permute-start(f32[160,128]{1,0:T(8,128)S(1)} %add_add_fusion.1), channel_id=1, source_target_pairs={{0,16},{8,24},{16,0},{24,8},{1,17},{9,25},{17,1},{25,9},{2,18},{10... | collective-permute-start | bytes 245768 | tf_op jit(solution)/shard_map/ppermute | solution.py:14
  93.6 3.6 %collective-permute-start.17 = (f32[160,128]{1,0:T(8,128)S(1)}, f32[160,128]{1,0:T(8,128)S(1)}, u32[]{:S(2)}, u32[]{:S(2)}) collective-permute-start(f32[160,128]{1,0:T(8,128)S(1)} %add_add_fusion.1), channel_id=1, source_target_pairs={{0,24},{8,0},{16,8},{24,16},{1,25},{9,1},{17,9},{25,17},{2,26},{10... | collective-permute-start | bytes 245768 | tf_op jit(solution)/shard_map/ppermute | solution.py:14
  97.2 6.8 %collective-permute-start.18 = (f32[160,128]{1,0:T(8,128)S(1)}, f32[160,128]{1,0:T(8,128)S(1)}, u32[]{:S(2)}, u32[]{:S(2)}) collective-permute-start(f32[160,128]{1,0:T(8,128)S(1)} %get-tuple-element.43), channel_id=1, source_target_pairs={{0,1},{1,64},{64,65},{65,0},{2,3},{3,66},{66,67},{67,2},{4,5},{5,6... | collective-permute-start | bytes 245768 | tf_op jit(solution)/shard_map/ppermute | solution.py:14
  97.9 6.7 %collective-permute-start.19 = (f32[160,128]{1,0:T(8,128)S(1)}, f32[160,128]{1,0:T(8,128)S(1)}, u32[]{:S(2)}, u32[]{:S(2)}) collective-permute-start(f32[160,128]{1,0:T(8,128)S(1)} %get-tuple-element.43), channel_id=1, source_target_pairs={{0,64},{1,65},{64,0},{65,1},{2,66},{3,67},{66,2},{67,3},{4,68},{5,... | collective-permute-start | bytes 245768 | tf_op jit(solution)/shard_map/ppermute | solution.py:14
  102.1 3.4 %collective-permute-start.20 = (f32[160,128]{1,0:T(8,128)S(1)}, f32[160,128]{1,0:T(8,128)S(1)}, u32[]{:S(2)}, u32[]{:S(2)}) collective-permute-start(f32[160,128]{1,0:T(8,128)S(1)} %get-tuple-element.43), channel_id=1, source_target_pairs={{0,65},{1,0},{64,1},{65,64},{2,67},{3,2},{66,3},{67,66},{4,69},{5,... | collective-permute-start | bytes 245768 | tf_op jit(solution)/shard_map/ppermute | solution.py:14
  105.5 5.4 %collective-permute-start.21 = (f32[4,160,128]{2,1,0:T(8,128)S(1)}, f32[4,160,128]{2,1,0:T(8,128)S(1)}, u32[]{:S(2)}, u32[]{:S(2)}) collective-permute-start(f32[4,160,128]{2,1,0:T(8,128)S(1)} %bitcast_dynamic-update-slice_fusion.2), channel_id=1, source_target_pairs={{0,32},{32,0},{1,33},{33,1},{2,34},{34,2},{3,35},{35,3},{4,36},{36... | collective-permute-start | bytes 983048 | tf_op jit(solution)/shard_map/ppermute | solution.py:14
  (8 other events, 30.7 us)
